TPU v7x, 32 devices: a whole 2x2x4 slice. The times are simulated.
32 devices in a mesh: wide: 16 (over z, y, core), narrow: 2 (over x).
Axes of the slice: x: 2, y: 2, z: 4, core: 2. Of those that a mesh axis runs over, the one named last changes fastest.
Arguments:
- target: bfloat16 [16, 512, 512], P('wide', 'narrow'), may hold values from -6 to 6
- memory: bfloat16 [16, 512, 512], P('wide', 'narrow'), may hold values from -6 to 6
- target_lens: int32 [16, 8], P('wide'), may hold values from 1 to 384, as said below
- source_lens: int32 [16, 8], P('wide'), may hold values from 1 to 384, as said below
- self_in: bfloat16 [512, 1536], replicated, may hold values from -0.25 to 0.25
- self_out: bfloat16 [512, 512], replicated, may hold values from -1 to 1
- cross_q: bfloat16 [512, 512], replicated, may hold values from -0.25 to 0.25
- cross_kv: bfloat16 [512, 1024], replicated, may hold values from -0.25 to 0.25
- cross_out: bfloat16 [512, 512], replicated, may hold values from -1 to 1
- ffn_in: bfloat16 [512, 2048], replicated, may hold values from -0.25 to 0.25
- ffn_in_bias: float32 [2048], replicated, may hold values from -3 to 3
- ffn_out: bfloat16 [2048, 512], replicated, may hold values from -0.125 to 0.125
- ffn_out_bias: float32 [512], replicated, may hold values from -3 to 3
- norm_gain: float32 [3, 512], replicated, may hold values from 0.1 to 1.9
- norm_bias: float32 [3, 512], replicated, may hold values from -3 to 3
- cotangent: bfloat16 [16, 512, 512], P('wide', 'narrow'), may hold values from -6 to 6
Outputs:
- output: bfloat16 [16, 512, 512], P('wide', 'narrow')
- target_grad: float32 [16, 512, 512], P('wide', 'narrow')
- memory_grad: float32 [16, 512, 512], P('wide', 'narrow')
- self_in_grad: float32 [512, 1536], P('narrow')
- self_out_grad: float32 [512, 512], P('narrow')
- cross_q_grad: float32 [512, 512], P('narrow')
- cross_kv_grad: float32 [512, 1024], P('narrow')
- cross_out_grad: float32 [512, 512], P('narrow')
- ffn_in_grad: float32 [512, 2048], P('narrow')
- ffn_in_bias_grad: float32 [2048], P('narrow')
- ffn_out_grad: float32 [2048, 512], P('narrow')
- ffn_out_bias_grad: float32 [512], P('narrow')
- norm_gain_grad: float32 [3, 512], P(None, 'narrow')
- norm_bias_grad: float32 [3, 512], P(None, 'narrow')
Inputs may be any that keep to these rules, and one draw needn't show every extreme that they name: `target_lens`: row b holds 8 target documents in order with these lengths; positions after their sum are padding. Target document j attends to source document j. `source_lens`: row b holds 8 source documents in order with these lengths; positions after their sum are padding.
All inputs are finite; a program needn't handle non-finite values.
Results may differ from a plain program's by a relative error of at most 0.025.
Values may be sent and summed in bfloat16 or wider, within the bound.
No kernel may reach another device: no remote copies, remote signals or barrier semaphores. Data moves between devices by JAX's collectives and lax.ppermute only.
A program may use at most 128 MiB of HBM per device.

v0:
```python
import functools
import math
import types

import jax
import jax.numpy as jnp
from jax import lax
from jax.experimental import pallas as pl
from jax.experimental.pallas import tpu as pltpu
from jax.sharding import PartitionSpec as P

HEADS = 8
HEAD_DIM = 64


EPSILON = 1e-05
MASKED = -1e30


def segment_ids(doc_lens, length):
    ends = jnp.cumsum(doc_lens, axis=-1)
    places = jnp.arange(length, dtype=jnp.int32)
    return jnp.sum((places[:, None] >= ends[..., None, :]).astype(jnp.int32), axis=-1)


def layer_norm(values, gain, shift):
    centre = values - jnp.mean(values, axis=-1, keepdims=True)
    spread = jnp.mean(centre * centre, axis=-1, keepdims=True)
    return centre * lax.rsqrt(spread + EPSILON) * gain + shift


def gelu_tanh(values):
    return jax.nn.gelu(values, approximate=True)


def project(activity, weight):
    return jnp.einsum("rsd,de->rse", activity, weight, preferred_element_type=jnp.float32)


def project_back(gradient, weight):
    return jnp.einsum("rse,de->rsd", gradient, weight, preferred_element_type=jnp.float32)


def weight_grad(activity, gradient):
    return jnp.einsum("rsd,rse->de", activity, gradient, preferred_element_type=jnp.float32)


def split_heads(values):
    return values.reshape(values.shape[0], values.shape[1], HEADS, HEAD_DIM)


def join_heads(values):
    return values.reshape(values.shape[0], values.shape[1], HEADS * HEAD_DIM)


def block_scores(query_heads, key_heads, query_seg, key_seg, query_pos, key_pos, causal):
    raw_scores = jnp.einsum(
        "rqhd,rkhd->rhqk", query_heads, key_heads, preferred_element_type=jnp.float32
    )
    visible = query_seg[:, :, None] == key_seg[:, None, :]
    if causal:
        visible = visible & (key_pos[None, None, :] <= query_pos[None, :, None])
    return jnp.where(visible[:, None], raw_scores * HEAD_DIM ** (-0.5), MASKED)


def block_backward(query_heads, grad_heads, key_heads, value_heads, scores, log_norm, row_dot):
    attention = jnp.exp(scores - log_norm[..., None])
    grad_attn = jnp.einsum(
        "rqhd,rkhd->rhqk", grad_heads, value_heads, preferred_element_type=jnp.float32
    )
    grad_scores = (attention * (grad_attn - row_dot[..., None]) * HEAD_DIM ** (-0.5)).astype(
        jnp.bfloat16
    )
    grad_query = jnp.einsum(
        "rhqk,rkhd->rqhd", grad_scores, key_heads, preferred_element_type=jnp.float32
    )
    grad_key = jnp.einsum(
        "rhqk,rqhd->rkhd", grad_scores, query_heads, preferred_element_type=jnp.float32
    )
    grad_value = jnp.einsum(
        "rhqk,rqhd->rkhd",
        attention.astype(jnp.bfloat16),
        grad_heads,
        preferred_element_type=jnp.float32,
    )
    return (grad_query, jnp.concatenate([join_heads(grad_key), join_heads(grad_value)], axis=-1))


def make_key_fold(query_heads, query_seg, key_seg_full, query_pos, causal, running, portion):
    run_max, run_sum, stored = running
    span_len = portion.shape[1]
    key_pos = jnp.arange(span_len, dtype=jnp.int32)
    scores = block_scores(
        query_heads,
        split_heads(portion[:, :, : HEADS * HEAD_DIM]),
        query_seg,
        key_seg_full,
        query_pos,
        key_pos,
        causal,
    )
    new_max = jnp.maximum(run_max, jnp.max(scores, axis=-1))
    run_sum = jnp.sum(jnp.exp(scores - new_max[..., None]), axis=-1)
    stored = portion
    return (new_max, run_sum, stored)


def attend_stored(query_heads, stored, query_seg, key_seg_full, query_pos, causal, log_norm):
    total_len = stored.shape[1]
    pair_half = stored.shape[2] // 2
    block_len = math.gcd(total_len, max(query_heads.shape[1], 512))

    def advance(low_sum, block_idx):
        begin_at = block_idx * block_len
        portion = lax.dynamic_slice_in_dim(stored, begin_at, block_len, 1)
        key_seg = lax.dynamic_slice_in_dim(key_seg_full, begin_at, block_len, 1)
        key_pos = begin_at + jnp.arange(block_len, dtype=jnp.int32)
        value_heads = split_heads(portion[:, :, pair_half:])
        scores = block_scores(
            query_heads,
            split_heads(portion[:, :, :pair_half]),
            query_seg,
            key_seg,
            query_pos,
            key_pos,
            causal,
        )
        attention = jnp.exp(scores - log_norm[..., None])
        low_sum = low_sum + jnp.einsum(
            "rhqk,rkhd->rqhd",
            attention.astype(jnp.bfloat16),
            value_heads,
            preferred_element_type=jnp.float32,
        )
        return (low_sum, None)

    zeros_q = jnp.zeros(query_heads.shape, jnp.float32)
    low_sum, _ = lax.scan(advance, zeros_q, jnp.arange(total_len // block_len, dtype=jnp.int32))
    return low_sum


def attend_back_stored(
    query_heads, grad_heads, stored, query_seg, key_seg_full, query_pos, causal, log_norm, row_dot
):
    total_len = stored.shape[1]
    pair_half = stored.shape[2] // 2
    block_len = math.gcd(total_len, max(query_heads.shape[1], 512))

    def advance(block_idx, running):
        grad_query, grad_term = running
        begin_at = block_idx * block_len
        portion = lax.dynamic_slice_in_dim(stored, begin_at, block_len, 1)
        key_seg = lax.dynamic_slice_in_dim(key_seg_full, begin_at, block_len, 1)
        key_pos = begin_at + jnp.arange(block_len, dtype=jnp.int32)
        key_heads = split_heads(portion[:, :, :pair_half])
        value_heads = split_heads(portion[:, :, pair_half:])
        scores = block_scores(
            query_heads, key_heads, query_seg, key_seg, query_pos, key_pos, causal
        )
        block_dq, block_dkv = block_backward(
            query_heads, grad_heads, key_heads, value_heads, scores, log_norm, row_dot
        )
        grad_term = lax.dynamic_update_slice_in_dim(grad_term, block_dkv, begin_at, 1)
        return (grad_query + block_dq, grad_term)

    start_vals = (jnp.zeros(query_heads.shape, jnp.float32), jnp.zeros(stored.shape, jnp.float32))
    grad_query, grad_term = lax.fori_loop(0, total_len // block_len, advance, start_vals)
    return (join_heads(grad_query), grad_term)


def local(
    target,
    memory,
    target_lens,
    source_lens,
    self_in,
    self_out,
    cross_q,
    cross_kv,
    cross_out,
    ffn_in,
    ffn_in_bias,
    ffn_out,
    ffn_out_bias,
    norm_gain,
    norm_bias,
    cotangent,
):
    row_count, shard_len, feat_width = target.shape
    total_len = shard_len * lax.axis_size("narrow")
    own_start = lax.axis_index("narrow") * shard_len
    own_pos = own_start + jnp.arange(shard_len, dtype=jnp.int32)
    target_seg = segment_ids(target_lens, total_len)
    source_seg = segment_ids(source_lens, total_len)
    target_own = lax.dynamic_slice_in_dim(target_seg, own_start, shard_len, 1)
    start_state = (
        jnp.full((row_count, HEADS, shard_len), MASKED, jnp.float32),
        jnp.zeros((row_count, HEADS, shard_len), jnp.float32),
        jnp.zeros((row_count, total_len, 2 * feat_width), jnp.bfloat16),
    )
    triple = project(target, self_in).astype(jnp.bfloat16)
    self_query = split_heads(triple[:, :, :feat_width])
    self_pairs = triple[:, :, feat_width:]
    self_max, self_sum, self_store = make_key_fold(
        self_query,
        target_own,
        target_seg,
        own_pos,
        True,
        start_state,
        lax.all_gather(self_pairs, "narrow", axis=1, tiled=True),
    )
    self_norm = self_max + jnp.log(self_sum)
    self_low = attend_stored(
        self_query, self_store, target_own, target_seg, own_pos, True, self_norm
    )
    self_mix = join_heads(self_low).astype(jnp.bfloat16)
    first, first_pull = jax.vjp(
        layer_norm,
        target.astype(jnp.float32) + project(self_mix, self_out),
        norm_gain[0],
        norm_bias[0],
    )
    first_low = first.astype(jnp.bfloat16)
    cross_query = split_heads(project(first_low, cross_q).astype(jnp.bfloat16))
    cross_pairs = project(memory, cross_kv).astype(jnp.bfloat16)
    cross_max, cross_sum, cross_store = make_key_fold(
        cross_query,
        target_own,
        source_seg,
        own_pos,
        False,
        start_state,
        lax.all_gather(cross_pairs, "narrow", axis=1, tiled=True),
    )
    cross_norm = cross_max + jnp.log(cross_sum)
    cross_low = attend_stored(
        cross_query, cross_store, target_own, source_seg, own_pos, False, cross_norm
    )
    cross_mix = join_heads(cross_low).astype(jnp.bfloat16)
    second, second_pull = jax.vjp(
        layer_norm, first + project(cross_mix, cross_out), norm_gain[1], norm_bias[1]
    )
    second_low = second.astype(jnp.bfloat16)
    inner = project(second_low, ffn_in) + ffn_in_bias
    active, gelu_pull = jax.vjp(gelu_tanh, inner)
    active_low = active.astype(jnp.bfloat16)
    result, third_pull = jax.vjp(
        layer_norm, second + project(active_low, ffn_out) + ffn_out_bias, norm_gain[2], norm_bias[2]
    )
    grad_third, gain_third, shift_third = third_pull(cotangent.astype(jnp.float32))
    grad_outer = grad_third.astype(jnp.bfloat16)
    ffn_out_g = weight_grad(active_low, grad_outer)
    ffn_out_bias_g = jnp.sum(grad_third, axis=(0, 1))
    (grad_active,) = gelu_pull(project_back(grad_outer, ffn_out))
    grad_inner = grad_active.astype(jnp.bfloat16)
    ffn_in_g = weight_grad(second_low, grad_inner)
    ffn_in_bias_g = jnp.sum(grad_active, axis=(0, 1))
    grad_second, gain_second, shift_second = second_pull(
        grad_third + project_back(grad_inner, ffn_in)
    )
    grad_cross = grad_second.astype(jnp.bfloat16)
    cross_out_g = weight_grad(cross_mix, grad_cross)
    cross_dout = split_heads(project_back(grad_cross, cross_out).astype(jnp.bfloat16))
    cross_dot = jnp.swapaxes(jnp.sum(cross_dout.astype(jnp.float32) * cross_low, axis=-1), 1, 2)
    cross_dq, cross_term = attend_back_stored(
        cross_query,
        cross_dout,
        cross_store,
        target_own,
        source_seg,
        own_pos,
        False,
        cross_norm,
        cross_dot,
    )
    cross_dpairs = lax.psum_scatter(
        cross_term.astype(jnp.bfloat16), "narrow", scatter_dimension=1, tiled=True
    )
    cross_dq_low = cross_dq.astype(jnp.bfloat16)
    cross_q_g = weight_grad(first_low, cross_dq_low)
    cross_kv_g = weight_grad(memory, cross_dpairs)
    memory_grad = project_back(cross_dpairs, cross_kv)
    grad_first, gain_first, shift_first = first_pull(
        grad_second + project_back(cross_dq_low, cross_q)
    )
    grad_self = grad_first.astype(jnp.bfloat16)
    self_out_g = weight_grad(self_mix, grad_self)
    self_dout = split_heads(project_back(grad_self, self_out).astype(jnp.bfloat16))
    self_dot = jnp.swapaxes(jnp.sum(self_dout.astype(jnp.float32) * self_low, axis=-1), 1, 2)
    self_dq, self_term = attend_back_stored(
        self_query,
        self_dout,
        self_store,
        target_own,
        target_seg,
        own_pos,
        True,
        self_norm,
        self_dot,
    )
    self_dpairs = lax.psum_scatter(
        self_term.astype(jnp.bfloat16), "narrow", scatter_dimension=1, tiled=True
    ).astype(jnp.float32)
    grad_triple = jnp.concatenate([self_dq, self_dpairs], axis=-1).astype(jnp.bfloat16)
    self_in_g = weight_grad(target, grad_triple)
    target_grad = grad_first + project_back(grad_triple, self_in)
    gain_g = jnp.stack([gain_first, gain_second, gain_third])
    shift_g = jnp.stack([shift_first, shift_second, shift_third])
    sh_a, sh_b, sh_c, sh_d, sh_e, sh_f, sh_g, sh_h, sh_i, sh_j, sh_k = (
        lax.psum_scatter(
            self_in_g.astype(jnp.bfloat16), "narrow", scatter_dimension=0, tiled=True
        ).astype(jnp.float32),
        lax.psum_scatter(
            self_out_g.astype(jnp.bfloat16), "narrow", scatter_dimension=0, tiled=True
        ).astype(jnp.float32),
        lax.psum_scatter(
            cross_q_g.astype(jnp.bfloat16), "narrow", scatter_dimension=0, tiled=True
        ).astype(jnp.float32),
        lax.psum_scatter(
            cross_kv_g.astype(jnp.bfloat16), "narrow", scatter_dimension=0, tiled=True
        ).astype(jnp.float32),
        lax.psum_scatter(
            cross_out_g.astype(jnp.bfloat16), "narrow", scatter_dimension=0, tiled=True
        ).astype(jnp.float32),
        lax.psum_scatter(
            ffn_in_g.astype(jnp.bfloat16), "narrow", scatter_dimension=0, tiled=True
        ).astype(jnp.float32),
        lax.psum_scatter(
            ffn_in_bias_g.astype(jnp.bfloat16), "narrow", scatter_dimension=0, tiled=True
        ).astype(jnp.float32),
        lax.psum_scatter(
            ffn_out_g.astype(jnp.bfloat16), "narrow", scatter_dimension=0, tiled=True
        ).astype(jnp.float32),
        lax.psum_scatter(
            ffn_out_bias_g.astype(jnp.bfloat16), "narrow", scatter_dimension=0, tiled=True
        ).astype(jnp.float32),
        lax.psum_scatter(
            gain_g.astype(jnp.bfloat16), "narrow", scatter_dimension=1, tiled=True
        ).astype(jnp.float32),
        lax.psum_scatter(
            shift_g.astype(jnp.bfloat16), "narrow", scatter_dimension=1, tiled=True
        ).astype(jnp.float32),
    )
    summed = (
        lax.psum(sh_a.astype(jnp.bfloat16), "wide").astype(jnp.float32),
        lax.psum(sh_b.astype(jnp.bfloat16), "wide").astype(jnp.float32),
        lax.psum(sh_c.astype(jnp.bfloat16), "wide").astype(jnp.float32),
        lax.psum(sh_d.astype(jnp.bfloat16), "wide").astype(jnp.float32),
        lax.psum(sh_e.astype(jnp.bfloat16), "wide").astype(jnp.float32),
        lax.psum(sh_f.astype(jnp.bfloat16), "wide").astype(jnp.float32),
        lax.psum(sh_g.astype(jnp.bfloat16), "wide").astype(jnp.float32),
        lax.psum(sh_h.astype(jnp.bfloat16), "wide").astype(jnp.float32),
        lax.psum(sh_i.astype(jnp.bfloat16), "wide").astype(jnp.float32),
        lax.psum(sh_j.astype(jnp.bfloat16), "wide").astype(jnp.float32),
        lax.psum(sh_k.astype(jnp.bfloat16), "wide").astype(jnp.float32),
    )
    return (
        result.astype(jnp.bfloat16),
        target_grad,
        memory_grad,
        summed[0],
        summed[1],
        summed[2],
        summed[3],
        summed[4],
        summed[5],
        summed[6],
        summed[7],
        summed[8],
        summed[9],
        summed[10],
    )


def dot_nn(left, right):
    return jnp.dot(left, right, preferred_element_type=jnp.float32)


def dot_nt(left, right):
    return lax.dot_general(left, right, (((1,), (1,)), ((), ())), preferred_element_type=jnp.float32)


def dot_tn(left, right):
    return lax.dot_general(left, right, (((0,), (0,)), ((), ())), preferred_element_type=jnp.float32)


def low(values):
    return values.astype(jnp.bfloat16)


def centred(values):
    return values - jnp.mean(values, axis=-1, keepdims=True)


def unit_of(centre):
    scale = lax.rsqrt(jnp.mean(centre * centre, axis=-1, keepdims=True) + EPSILON)
    return centre * scale, scale


def normalize_back(grad, gain, unit, scale):
    inner = grad * gain
    return scale * (
        inner
        - jnp.mean(inner, axis=-1, keepdims=True)
        - unit * jnp.mean(inner * unit, axis=-1, keepdims=True)
    )


DOCUMENTS = 8
TARGET_LENS = range(3, 3 + DOCUMENTS)
SOURCE_LENS = range(3 + DOCUMENTS, 3 + 2 * DOCUMENTS)


def seg_along(place_ref, lens, shape, dim):
    places = lax.broadcasted_iota(jnp.int32, shape, dim)
    seg = jnp.zeros(shape, jnp.int32)
    end = jnp.int32(0)
    for doc in lens:
        end = end + place_ref[doc]
        seg = seg + (places >= end).astype(jnp.int32)
    return seg


def visible_pairs(place_ref, query_lens, key_lens, length, causal):
    query_seg = seg_along(place_ref, query_lens, (length, 1), 0)
    seen = query_seg == seg_along(place_ref, key_lens, (1, length), 1)
    if causal:
        rows = lax.broadcasted_iota(jnp.int32, (length, length), 0)
        cols = lax.broadcasted_iota(jnp.int32, (length, length), 1)
        seen = seen & (cols <= rows)
    return seen


class Far:
    def __init__(self, far_refs, near, sems, parts, inward):
        self.near, self.sems, self.inward, self.waited = near, sems, inward, set()
        self.far_refs, self.parts = far_refs, parts

    def copy(self, part):
        far, near = self.far_refs[0 if len(self.far_refs) == 1 else part], self.near
        if self.parts is not None:
            far_at, near_at = self.parts(part)
            far = far if far_at is None else far.at[far_at]
            near = near if near_at is None else near.at[near_at]
        ends = (far, near) if self.inward else (near, far)
        return pltpu.make_async_copy(*ends, self.sems.at[part])

    def start(self):
        for part in range(self.sems.shape[0]):
            self.copy(part).start()

    def wait(self):
        for part in range(self.sems.shape[0]):
            self.copy(part).wait()

    def get(self):
        if 0 not in self.waited:
            self.waited.add(0)
            self.wait()
        return self.near


TOKEN = (8, 128)
SMALL_COST = 25 * 10**9


def write_token(place_ref):
    lane = lax.broadcasted_iota(jnp.int32, TOKEN, 1)
    token = jnp.zeros(TOKEN, jnp.int32)
    for index in range(3):
        token = jnp.where(lane == index, place_ref[index], token)
    return token


class Chain:
    def __init__(self):
        self.token = None


class Kernel:
    def __init__(self, chain, place, *scalars):
        self.chain = chain
        self.scalars = (place, *scalars)
        self.operands, self.results, self.scratch, self.entries = [], [], [], {}
        self.place = place

    def _scratch(self, what):
        self.scratch.append(what)
        return ("scratch", len(self.scratch) - 1)

    def _operand(self, array, space):
        if space is not pl.ANY:
            array = pltpu.with_memory_space_constraint(array, space)
        self.operands.append((array, space))
        return ("operand", len(self.operands) - 1)

    def _result(self, shape, dtype, space):
        kept = jax.ShapeDtypeStruct(shape, dtype) if space is pl.ANY else space(shape, dtype)
        self.results.append((kept, space))
        return ("result", len(self.results) - 1)

    def near(self, **arrays):
        for name, array in arrays.items():
            self.entries[name] = ("plain", self._operand(array, pltpu.VMEM))

    def far(self, **arrays):
        for name, array in arrays.items():
            ref = self._operand(array, pltpu.HBM)
            near = self._scratch(pltpu.VMEM(array.shape, array.dtype))
            self.entries[name] = ("far", [ref], near, self._scratch(pltpu.SemaphoreType.DMA((1,))), "all", True)

    def halves(self, **pairs):
        for name, (own, other) in pairs.items():
            refs = [self._operand(own, pltpu.HBM), self._operand(other, pl.ANY)]
            near = self._scratch(pltpu.VMEM((2 * own.shape[0], own.shape[1]), own.dtype))
            self.entries[name] = ("far", refs, near, self._scratch(pltpu.SemaphoreType.DMA((2,))), "halves", True)

    def heads(self, name, array, first, last):
        ref = self._operand(array, pltpu.HBM)
        near = self._scratch(pltpu.VMEM((2 * (last - first),) + array.shape[1:], array.dtype))
        sems = self._scratch(pltpu.SemaphoreType.DMA((last - first,)))
        self.entries[name] = ("far", [ref], near, sems, ("heads", first), True)

    def near_out(self, **outs):
        for name, (shape, dtype) in outs.items():
            self.entries[name] = ("plain", self._result(shape, dtype, pltpu.VMEM))

    def free_out(self, **outs):
        for name, (shape, dtype) in outs.items():
            ref = self._result(shape, dtype, pl.ANY)
            near = self._scratch(pltpu.VMEM(shape, dtype))
            self.entries[name] = ("far", [ref], near, self._scratch(pltpu.SemaphoreType.DMA((1,))), "all", False)

    def far_out(self, **outs):
        for name, (shape, dtype) in outs.items():
            ref = self._result(shape, dtype, pltpu.HBM)
            near = self._scratch(pltpu.VMEM(shape, dtype))
            self.entries[name] = ("far", [ref], near, self._scratch(pltpu.SemaphoreType.DMA((1,))), "all", False)

    def heads_out(self, **outs):
        for name, (shape, dtype) in outs.items():
            ref = self._result(shape, dtype, pltpu.HBM)
            near = self._scratch(pltpu.VMEM(shape, dtype))
            sems = self._scratch(pltpu.SemaphoreType.DMA((shape[0] // 2,)))
            self.entries[name] = ("far", [ref], near, sems, ("heads", 0), False)

    def copy_out(self, **outs):
        for name, (source, shape, dtype) in outs.items():
            ref = self._result(shape, dtype, pltpu.HBM)
            near = self.entries[source][1]
            self.entries[name] = ("far", [ref], near, self._scratch(pltpu.SemaphoreType.DMA((1,))), "all", False)

    def prefetch(self, **arrays):
        for name, array in arrays.items():
            ref = self._operand(array, pltpu.HBM)
            near = self._result(array.shape, array.dtype, pltpu.VMEM)
            sems = self._scratch(pltpu.SemaphoreType.DMA((1,)))
            self.entries["prefetch_" + name] = ("far", [ref], near, sems, "all", True)

    def hold(self, **outs):
        for name, (shape, dtype) in outs.items():
            self.entries[name] = ("plain", self._scratch(pltpu.VMEM(shape, dtype)))

    def run(self, body, flops, vmem_mib):
        held = None if self.chain.token is None else self._operand(self.chain.token, pltpu.VMEM)[1]
        last = self._result(TOKEN, jnp.int32, pltpu.VMEM)[1]

        def kernel(*refs):
            count = len(self.scalars)
            bounds = (count, count + len(self.operands), count + len(self.operands) + len(self.results))
            groups = {
                "operand": refs[bounds[0] : bounds[1]],
                "result": refs[bounds[1] : bounds[2]],
                "scratch": refs[bounds[2] :],
            }
            mine = refs[0][0]
            views = types.SimpleNamespace()
            for name, entry in self.entries.items():
                if entry[0] == "plain":
                    setattr(views, name, groups[entry[1][0]][entry[1][1]])
                    continue
                _, far, near, sems, cut, inward = entry
                near = groups[near[0]][near[1]]
                half = near.shape[0] // 2
                parts = None
                if cut == "halves":

                    def parts(part, half=half):
                        place = mine if part == 0 else 1 - mine
                        return (None, pl.ds(pl.multiple_of(place * half, half), half))

                if isinstance(cut, tuple):

                    def parts(part, skip=cut[1]):
                        return (pl.ds((skip + part) * 2, 2), pl.ds(part * 2, 2))

                setattr(views, name, Far([groups[g][i] for g, i in far], near, groups[sems[0]][sems[1]], parts, inward))
            groups["result"][last][...] = write_token(refs[0]) if held is None else groups["operand"][held][...]
            for view in vars(views).values():
                if isinstance(view, Far) and view.inward:
                    view.start()
            body(refs[:count], views)
            for name, view in vars(views).items():
                if isinstance(view, Far) and (not view.inward or name.startswith("prefetch_")):
                    view.get()

        arrays = [array for array, _ in self.operands]
        shapes = [kept for kept, _ in self.results]
        moved = sum(math.prod(a.shape) * a.dtype.itemsize for a in arrays)
        *results, self.chain.token = pl.pallas_call(
            kernel,
            out_shape=shapes,
            in_specs=[pl.BlockSpec(memory_space=pltpu.SMEM)] * len(self.scalars)
            + [pl.BlockSpec(memory_space=space) for _, space in self.operands],
            out_specs=[pl.BlockSpec(memory_space=space) for _, space in self.results],
            scratch_shapes=self.scratch,
            compiler_params=pltpu.CompilerParams(vmem_limit_bytes=vmem_mib * 2**20),
            cost_estimate=pl.CostEstimate(flops=flops, bytes_accessed=moved, transcendentals=0),
        )(*self.scalars, *arrays)
        return results


def ref_of(view):
    return view.get() if isinstance(view, Far) else view


def near_of(view):
    return view.near if isinstance(view, Far) else view


def own_columns(ref, start, width):
    return ref[:, pl.ds(pl.multiple_of(start, 128), width)]


def grad_rows(place_ref, activity_ref, grads, keep_ref, send_ref, col):
    rows = keep_ref.shape[0]
    first = place_ref[0] * 2 * rows
    for ref, part in ((keep_ref, place_ref[1]), (send_ref, 1 - place_ref[1])):
        piece = own_columns(activity_ref, first + part * rows, rows)
        at = col
        for grad in grads:
            ref[:, at : at + grad.shape[1]] = dot_tn(piece, grad).astype(ref.dtype)
            at += grad.shape[1]


def query_blocks(length, causal):
    if causal:
        return ((0, length // 2, length // 2), (length // 2, length, length))
    return ((0, length // 2, length), (length // 2, length, length))


PAIR = 2 * HEAD_DIM


def head_lanes():
    lane = lax.broadcasted_iota(jnp.int32, (1, PAIR), 1)
    return (lane < HEAD_DIM, lane >= HEAD_DIM)


def attend_all(query_ref, key_ref, value_ref, bias_ref, attn, mix_ref, causal):
    length = query_ref.shape[0]

    def one_pair(pair, carry):
        lanes = pl.ds(pl.multiple_of(pair * PAIR, PAIR), PAIR)
        keys, values = key_ref[:, lanes], value_ref[:, lanes]
        zero = jnp.zeros_like(keys)
        for begin, end, reach in query_blocks(length, causal):
            queries = query_ref[begin:end, lanes]
            total = jnp.zeros((end - begin, PAIR), jnp.float32)
            for sub, inside in enumerate(head_lanes()):
                scores = dot_nt(queries, jnp.where(inside, keys, zero)[:reach])
                scores = scores + bias_ref[begin:end, :reach]
                weights = jnp.exp(scores - jnp.max(scores, axis=-1, keepdims=True))
                weights = low(weights * (1.0 / jnp.sum(weights, axis=-1, keepdims=True)))
                attn.near[pair * 2 + sub, begin:end, :reach] = weights
                if reach < length:
                    attn.near[pair * 2 + sub, begin:end, reach:] = jnp.zeros((end - begin, length - reach), weights.dtype)
                total = total + dot_nn(weights, jnp.where(inside, values, zero)[:reach])
            mix_ref[begin:end, lanes] = low(total)
        attn.copy(pair).start()
        return carry

    lax.fori_loop(0, HEADS // 2, one_pair, 0, unroll=True)


def attend_all_back(
    pairs, query_ref, query_t_ref, key_ref, value_ref, attn, mix_ref, grad_ref, grad_t_ref, dquery_ref, dpairs_t_ref, causal
):
    length = query_ref.shape[0]
    width = grad_ref.shape[1]

    def one_pair(pair, carry):
        place = pair - pairs[0]
        lanes = pl.ds(pl.multiple_of(pair * PAIR, PAIR), PAIR)
        near_lanes = pl.ds(pl.multiple_of(place * PAIR, PAIR), PAIR)
        attn.copy(place).wait()
        keys, values = key_ref[:, lanes], value_ref[:, lanes]
        zero = jnp.zeros_like(keys)
        blocks = query_blocks(length, causal)
        dquery = [jnp.zeros((end - begin, PAIR), jnp.float32) for begin, end, _ in blocks]
        for sub, inside in enumerate(head_lanes()):
            head_keys = jnp.where(inside, keys, zero)
            head_values = jnp.where(inside, values, zero)
            rows = pl.ds(pl.multiple_of(place * PAIR + sub * HEAD_DIM, HEAD_DIM), HEAD_DIM)
            parts = []
            for idx, (begin, end, reach) in enumerate(blocks):
                grads = grad_ref[begin:end, near_lanes]
                dots = grads.astype(jnp.float32) * mix_ref[begin:end, lanes].astype(jnp.float32)
                row_dot = jnp.sum(jnp.where(inside, dots, 0.0), axis=-1, keepdims=True)
                weights = attn.near[place * 2 + sub, begin:end, :reach]
                dattn = dot_nt(grads, head_values[:reach])
                dscores = low(weights.astype(jnp.float32) * (dattn - row_dot))
                dquery[idx] = dquery[idx] + dot_nn(dscores, head_keys[:reach])
                dkey_t = dot_nn(query_t_ref[rows, begin:end], dscores)
                dvalue_t = dot_nn(grad_t_ref[rows, begin:end], weights)
                parts.append((reach, dkey_t, dvalue_t))
            (reach, dkey_t, dvalue_t), (_, dkey_more, dvalue_more) = parts
            rows_v = pl.ds(pl.multiple_of(width + place * PAIR + sub * HEAD_DIM, HEAD_DIM), HEAD_DIM)
            for where, less, more in ((rows, dkey_t, dkey_more), (rows_v, dvalue_t, dvalue_more)):
                dpairs_t_ref[where, :reach] = low(less + more[:, :reach])
                if reach < length:
                    dpairs_t_ref[where, reach:] = low(more[:, reach:])
        for (begin, end, _), dq in zip(blocks, dquery):
            dquery_ref[begin:end, near_lanes] = low(dq * HEAD_DIM ** (-0.5))
        return carry

    lax.fori_loop(pairs[0], pairs[1], one_pair, 0)


def scaled_query(values):
    return low(low(values) * jnp.bfloat16(HEAD_DIM ** (-0.5)))


def gain_of(vectors_ref, layer):
    return vectors_ref[layer : layer + 1, :]


def shift_of(vectors_ref, layer):
    return vectors_ref[3 + layer : 4 + layer, :]


def first_body(scalars, views):
    (place_ref,) = scalars
    length = views.self_bias.shape[0]
    own, triple = views.own.get(), views.triple_own
    width = own.shape[1]
    weight_ref = views.prefetch_self_in.near
    views.self_bias[...] = jnp.where(visible_pairs(place_ref, TARGET_LENS, TARGET_LENS, length, True), 0.0, MASKED)
    views.cross_bias[...] = jnp.where(visible_pairs(place_ref, TARGET_LENS, SOURCE_LENS, length, False), 0.0, MASKED)
    views.prefetch_self_in.get()
    triple[:, :width] = scaled_query(dot_nn(own[...], weight_ref[:, :width]))
    triple[:, width:] = low(dot_nn(own[...], weight_ref[:, width:]))


def self_forward_body(scalars, views):
    place_ref, = scalars
    other_ref, weight_ref = views.other, views.self_in
    triple, mix = views.triple, views.mix
    half, width = other_ref.shape
    own_rows, other_rows = rows_at(place_ref[0], half), rows_at(1 - place_ref[0], half)
    triple.near[own_rows, :] = views.triple_own[...]
    triple.near[other_rows, :width] = scaled_query(dot_nn(other_ref[...], weight_ref[:, :width]))
    triple.near[other_rows, width:] = low(dot_nn(other_ref[...], weight_ref[:, width:]))
    triple.start()
    attend_all(
        triple.near.at[:, :width], triple.near.at[:, width : 2 * width], triple.near.at[:, 2 * width :],
        views.bias, views.attn, mix.near, True,
    )
    mix.start()
    centre_ref = views.centre_first
    for rows, part_ref in ((own_rows, views.own), (other_rows, other_ref)):
        summed = part_ref[...].astype(jnp.float32) + dot_nn(mix.near[rows, :], views.self_out[...])
        centre_ref[rows, :] = centred(summed)


def cross_forward_body(scalars, views):
    query, pairs, mix = views.query, views.pairs, views.mix
    width = mix.near.shape[1]
    bias_ref, centre_first_ref, vectors_ref = views.bias, views.centre_first, views.vectors
    views.centre_first_far.start()
    first = unit_of(centre_first_ref[...])[0] * gain_of(vectors_ref, 0) + shift_of(vectors_ref, 0)
    query.near[...] = scaled_query(dot_nn(low(first), views.cross_q[...]))
    query.start()
    pairs.near[...] = low(dot_nn(views.memory.get()[...], views.cross_kv[...]))
    pairs.start()
    attend_all(query.near, pairs.near.at[:, :width], pairs.near.at[:, width:], bias_ref, views.attn, mix.near, False)
    mix.start()
    first = unit_of(centre_first_ref[...])[0] * gain_of(vectors_ref, 0) + shift_of(vectors_ref, 0)
    views.centre_second[...] = centred(first + dot_nn(mix.near[...], views.cross_out[...]))


GELU_SCALE = math.sqrt(2.0 / math.pi)
GELU_CUBE = 0.044715


def gelu_both(values):
    square = values * values
    half = 0.5 * jnp.tanh(values * (GELU_SCALE + (GELU_SCALE * GELU_CUBE) * square)) + 0.5
    rise = values * (2.0 * GELU_SCALE + (6.0 * GELU_SCALE * GELU_CUBE) * square)
    return values * half, half + half * (1.0 - half) * rise


def feed_body(scalars, views):
    (place_ref,) = scalars
    length, width = views.centre_second.shape
    half = length // 2
    second_ref, active_ref, slope_ref = views.second, views.active, views.slope
    outer_ref, inner_ref, work_ref = views.outer, views.inner, views.grad_second
    vectors_ref = views.vectors
    second = unit_of(views.centre_second[...])[0] * gain_of(vectors_ref, 1) + shift_of(vectors_ref, 1)
    second_ref[...] = low(second)
    total = second + vectors_ref[6:7, :]
    in_ref, out_ref = views.ffn_in, views.ffn_out
    hidden = in_ref.shape[1]
    block = width
    for begin in range(0, hidden, block):
        cols = slice(begin, begin + block)
        inner = dot_nn(second_ref[...], in_ref[:, cols]) + vectors_ref[8 + begin // block : 9 + begin // block, :]
        active, slope_ref[:, cols] = gelu_both(inner)
        active_ref[:, cols] = low(active)
        total = total + dot_nn(active_ref[:, cols], out_ref[cols, :])
    unit, scale = unit_of(centred(total))
    work_ref[...] = unit * gain_of(vectors_ref, 2) + shift_of(vectors_ref, 2)
    views.output.near[...] = low(work_ref[pl.ds(pl.multiple_of(place_ref[0] * half, half), half), :])
    views.output.start()
    cotangent = views.cotangent.get()[...].astype(jnp.float32)
    sums_ref, wide_ref = views.sums, views.in_sums
    sums_ref[0:1, :] = jnp.sum(cotangent * unit, axis=0, keepdims=True)
    sums_ref[1:2, :] = jnp.sum(cotangent, axis=0, keepdims=True)
    grad_third = normalize_back(cotangent, gain_of(vectors_ref, 2), unit, scale)
    sums_ref[2:3, :] = jnp.sum(grad_third, axis=0, keepdims=True)
    outer_ref[...] = low(grad_third)
    work_ref[...] = grad_third
    keep, send = views.keep, views.send
    rows = keep.shape[0]
    groups = hidden // width
    for group in range(groups):
        cols = slice(group * width, (group + 1) * width)
        first = (place_ref[0] * groups + group) * 2 * rows
        for view, part in ((keep, place_ref[1]), (send, 1 - place_ref[1])):
            piece = own_columns(active_ref, first + part * rows, rows)
            view[:, cols] = dot_tn(piece, outer_ref[...]).astype(view.dtype)
    into_second = jnp.zeros((length, width), jnp.float32)
    for begin in range(0, hidden, block):
        cols = slice(begin, begin + block)
        grad_inner = dot_nt(outer_ref[...], out_ref[cols, :]) * slope_ref[:, cols]
        wide_ref[:, cols] = jnp.sum(grad_inner, axis=0, keepdims=True)
        inner_ref[:, cols] = low(grad_inner)
        into_second = into_second + dot_nt(inner_ref[:, cols], in_ref[:, cols])
    grad_rows(place_ref, second_ref, (inner_ref[...],), keep, send, hidden)
    work_ref[...] = work_ref[...] + into_second


def between_body(scalars, views):
    (place_ref,) = scalars
    length, width = views.grad.shape
    sums_ref, wide_ref, vectors_ref, small_ref = views.sums, views.in_sums, views.vectors, views.small
    work_ref = views.work
    grad = views.grad[...]
    unit_second, scale_second = unit_of(views.centre_second[...])
    grad_second = normalize_back(grad, gain_of(vectors_ref, 1), unit_second, scale_second)
    views.grad_second[...] = grad_second
    grad_low_ref = views.grad_low
    grad_low_ref[...] = low(grad_second)
    out_ref = views.cross_out
    seen = jnp.where(visible_pairs(place_ref, TARGET_LENS, SOURCE_LENS, length, False), 1.0, 0.0)
    seen = jnp.max(seen, axis=-1, keepdims=True)
    views.dmix[...] = low(dot_nt(grad_low_ref[...], out_ref[...]) * seen)
    views.dmix_t[...] = low(dot_nt(out_ref[...], grad_low_ref[...]))
    views.query_t[...] = views.query[...].T
    work_ref[0:3, :] = sums_ref[0:3, :]
    work_ref[3:4, :] = jnp.sum(grad * unit_second, axis=0, keepdims=True)
    work_ref[4:5, :] = jnp.sum(grad, axis=0, keepdims=True)
    columns = width // 2
    hidden = wide_ref.shape[1]
    small_ref[...] = jnp.zeros(small_ref.shape, jnp.float32)
    for row in range(5):
        small_ref[row : row + 1, :] = own_columns(work_ref.at[row : row + 1, :], place_ref[0] * columns, columns)
    for row in range(hidden // width):
        start = place_ref[0] * (hidden // 2) + row * columns
        small_ref[8 + row : 9 + row, :] = own_columns(wide_ref, start, columns)


def cross_back_body(scalars, views):
    (place_ref,) = scalars
    length, width = views.grad_second.shape
    half = length // 2
    first_ref, grad_ref, dmix_ref, dmix_t_ref = views.first, views.grad, views.dmix, views.dmix_t
    query_t_ref, dquery_ref, dpairs_t_ref = views.query_t, views.dquery, views.dpairs_t
    grad_second_ref = views.grad_second
    query_ref = views.query
    pairs_ref, mix_ref = views.pairs, views.mix
    attend_all_back(
        (0, HEADS // 2), query_ref, query_t_ref, pairs_ref.at[:, :width], pairs_ref.at[:, width:], views.attn, mix_ref,
        dmix_ref, dmix_t_ref, dquery_ref, dpairs_t_ref, False,
    )
    vectors_ref = views.vectors
    unit_first, scale_first = unit_of(views.centre_first.get()[...])
    first_ref[...] = low(unit_first * gain_of(vectors_ref, 0) + shift_of(vectors_ref, 0))
    memory_grad = views.memory_grad
    own_dpairs = own_columns(dpairs_t_ref, place_ref[0] * half, half).T
    memory_grad.near[...] = dot_nt(own_dpairs, views.cross_kv.get()[...])
    memory_grad.start()
    keep, send = views.keep, views.send
    grad_rows(place_ref, first_ref, (dquery_ref[...],), keep, send, 0)
    grad_rows(place_ref, views.memory.get(), (dpairs_t_ref[...].T,), keep, send, width)
    grad_rows(place_ref, mix_ref, (views.grad_low[...],), keep, send, 3 * width)
    grad = grad_second_ref[...] + dot_nt(dquery_ref[...], views.cross_q.get()[...])
    sums_ref, small_ref = views.sums, views.small
    sums_ref[0:1, :] = jnp.sum(grad * unit_first, axis=0, keepdims=True)
    sums_ref[1:2, :] = jnp.sum(grad, axis=0, keepdims=True)
    columns = width // 2
    turned_ref = views.turned
    turned_ref[...] = jnp.zeros(turned_ref.shape, jnp.float32)
    turned_ref[: small_ref.shape[0], :] = small_ref[...]
    for row in range(2):
        turned_ref[5 + row : 6 + row, :] = own_columns(sums_ref.at[row : row + 1, :], place_ref[0] * columns, columns)
    grad_first = normalize_back(grad, gain_of(vectors_ref, 0), unit_first, scale_first)
    views.grad_first[...] = grad_first
    grad_ref[...] = low(grad_first)
    grad_rows(place_ref, views.self_mix.get(), (grad_ref[...],), keep, send, 4 * width)
    rows = keep.shape[0]
    for ref, part in ((keep, place_ref[1]), (send, 1 - place_ref[1])):
        ref[:, 5 * width :] = own_columns(turned_ref, part * rows, rows).T.astype(ref.dtype)


def self_back_body(pairs, scalars, views):
    (place_ref,) = scalars
    length, width = views.grad_first.shape
    half = length // 2
    grad_ref, dmix_ref, dmix_t_ref = views.grad, views.dmix, views.dmix_t
    query_t_ref, dquery_ref, dpairs_t_ref = views.query_t, views.dquery, views.dpairs_t
    first, last = pairs[0] * PAIR, pairs[1] * PAIR
    span = last - first
    grad_ref[...] = low(views.grad_first[...])
    out_ref = views.self_out
    dmix_ref[...] = low(dot_nt(grad_ref[...], out_ref[first:last, :]))
    dmix_t_ref[...] = low(dot_nt(out_ref[first:last, :], grad_ref[...]))
    triple_ref = views.triple
    query_t_ref[...] = triple_ref[:, first:last].T
    attend_all_back(
        pairs, triple_ref.at[:, :width], query_t_ref, triple_ref.at[:, width : 2 * width], triple_ref.at[:, 2 * width :],
        views.attn, views.mix, dmix_ref, dmix_t_ref, dquery_ref, dpairs_t_ref, True,
    )
    own_rows = pl.ds(pl.multiple_of(place_ref[0] * half, half), half)
    own_dpairs = own_columns(dpairs_t_ref, place_ref[0] * half, half).T
    weight_ref = views.self_in.get()
    total = (
        dot_nt(dquery_ref[own_rows, :], weight_ref[:, first:last])
        + dot_nt(own_dpairs[:, :span], weight_ref[:, width + first : width + last])
        + dot_nt(own_dpairs[:, span:], weight_ref[:, 2 * width + first : 2 * width + last])
    )
    total = total + views.grad_first[own_rows, :]
    views.target_grad.near[...] = total
    views.target_grad.start()
    keep, send = views.keep, views.send
    grad_rows(place_ref, ref_of(views.target), (dquery_ref[...], dpairs_t_ref[...].T), keep, send, 0)


def send_wide(values, bit):
    count = lax.axis_size("wide")
    return lax.ppermute(values, "wide", [(i, i ^ (1 << bit)) for i in range(count)])


def bit_of(token_ref, bit):
    return (token_ref[0, 2] >> bit) & 1


def small_kernel(chain, body, arrays, outs):
    token = pltpu.with_memory_space_constraint(chain.token, pltpu.VMEM)

    def kernel(token_ref, *refs):
        *refs, last_ref = refs
        last_ref[...] = token_ref[...]
        body(token_ref, *refs)

    *results, chain.token = pl.pallas_call(
        kernel,
        out_shape=[jax.ShapeDtypeStruct(shape, dtype) for shape, dtype in outs] + [pltpu.VMEM(TOKEN, jnp.int32)],
        in_specs=[pl.BlockSpec(memory_space=pltpu.VMEM)] * (len(arrays) + 1),
        out_specs=[pl.BlockSpec(memory_space=pltpu.VMEM)] * (len(outs) + 1),
        compiler_params=pltpu.CompilerParams(vmem_limit_bytes=12 * 2**20),
        cost_estimate=pl.CostEstimate(flops=SMALL_COST, bytes_accessed=1, transcendentals=0),
    )(token, *arrays)
    return results


def rows_at(start, rows):
    return pl.ds(pl.multiple_of(start * rows, rows), rows)


def add_split(chain, keep, received, bit):
    rows = keep.shape[0] // 2
    shape = (rows,) + keep.shape[1:]

    def body(token_ref, keep_ref, came_ref, mine_ref, send_ref):
        mine = bit_of(token_ref, bit)
        for out, part in ((mine_ref, mine), (send_ref, 1 - mine)):
            where = rows_at(part, rows)
            out[...] = (keep_ref[where, :].astype(jnp.float32) + came_ref[where, :].astype(jnp.float32)).astype(out.dtype)

    outs = [(shape, jnp.float32), (shape, jnp.bfloat16)]
    return small_kernel(chain, body, (keep, received), outs)


def add_low(chain, keep, received):
    def body(token_ref, keep_ref, came_ref, out_ref):
        out_ref[...] = low(keep_ref[...].astype(jnp.float32) + came_ref[...].astype(jnp.float32))

    return small_kernel(chain, body, (keep, received), [(keep.shape, jnp.bfloat16)])[0]


def join_rows(chain, piece, received, bit):
    rows = piece.shape[0]

    def body(token_ref, own_ref, came_ref, out_ref):
        mine = bit_of(token_ref, bit)
        out_ref[rows_at(mine, rows), :] = own_ref[...]
        out_ref[rows_at(1 - mine, rows), :] = came_ref[...]

    shape = (2 * rows,) + piece.shape[1:]
    return small_kernel(chain, body, (piece, received), [(shape, piece.dtype)])[0]


def finish(chain, piece, received, cuts, outs, vectors=None):
    rows = piece.shape[0]

    def body(token_ref, *refs):
        core = token_ref[0, 1]
        for step in range(2):
            part = core ^ step
            for out, row, col, begin, size in cuts:
                where = pl.ds(pl.multiple_of(row + part * rows, rows), rows)
                refs[2 + out][where, col : col + size] = refs[step][:, begin : begin + size].astype(jnp.float32)
        if vectors:
            last = refs[0].shape[1] - 128
            turned = [refs[step][:, last:].astype(jnp.float32).T for step in range(2)]
            swap = core == 1
            turned = jnp.concatenate(
                [jnp.where(swap, turned[1], turned[0]), jnp.where(swap, turned[0], turned[1])], axis=1
            )
            for out, row, col, index in vectors:
                refs[2 + out][row : row + 1, col : col + 2 * rows] = turned[index : index + 1, :]

    return small_kernel(chain, body, (piece, received), outs)


HALVE, WHOLE, DOUBLE = range(3)


def rounds_of(bits):
    return [(HALVE, bit) for bit in bits[:-1]] + [(WHOLE, bits[-1])] + [(DOUBLE, bit) for bit in reversed(bits[:-1])]


class Chunk:
    def __init__(self, chain, keep, send, rounds):
        self.chain = chain
        self.kept, self.send = keep, send
        self.rounds, self.at = rounds, 0
        self.launch()

    def launch(self):
        self.received = send_wide(self.send, self.rounds[self.at][1])

    def advance(self):
        kind, bit = self.rounds[self.at]
        self.at += 1
        following, next_bit = self.rounds[self.at]
        if kind == DOUBLE:
            self.kept = self.send = join_rows(self.chain, self.kept, self.received, bit)
        elif following == HALVE:
            self.kept, self.send = add_split(self.chain, self.kept, self.received, next_bit)
        else:
            self.kept = self.send = add_low(self.chain, self.kept, self.received)
        self.launch()

    def left(self):
        return len(self.rounds) - 1 - self.at

    def finish(self, cuts, outs, vectors=None):
        return finish(self.chain, self.kept, self.received, cuts, outs, vectors)


def near_first(bits):
    return rounds_of(list(range(bits)))


def mid_first(bits):
    return rounds_of([0, 2, 1] + list(range(3, bits)))


def far_first(bits):
    return rounds_of([0] + list(range(2, bits)) + [1])


ORDER = dict(a=near_first, c=near_first, d=near_first)
SCHEDULE = ("a", "aca", "cadcadcdcdadcacdd")


def whole_rows(
    target, memory, target_lens, source_lens, self_in, self_out, cross_q, cross_kv, cross_out, ffn_in, ffn_in_bias,
    ffn_out, ffn_out_bias, norm_gain, norm_bias, cotangent,
):
    f32, bf16 = jnp.float32, jnp.bfloat16
    _, half, width = target.shape
    length = 2 * half
    hidden = ffn_in.shape[1]
    wide = lax.axis_index("wide")
    place = jnp.stack([lax.axis_index("narrow"), wide % 2, wide]).astype(jnp.int32)
    place = jnp.concatenate([place, target_lens[0], source_lens[0]])
    chain = Chain()

    def other_half(values):
        return lax.ppermute(values, "narrow", [(0, 1), (1, 0)])

    own_t, own_m, own_c = target[0], memory[0], cotangent[0]
    other_t, other_m, other_c = other_half(own_t), other_half(own_m), other_half(own_c)
    square = (length, width)
    attn_shape = (HEADS, length, length)
    macs = length * width * width
    rows = width // 4

    vectors = jnp.concatenate(
        [norm_gain, norm_bias, ffn_out_bias[None], jnp.zeros((1, width), f32), ffn_in_bias.reshape(-1, width)], axis=0
    )
    vectors = jnp.pad(vectors, ((0, -vectors.shape[0] % 8), (0, 0)))

    step = Kernel(chain, place)
    step.far(own=own_t)
    step.prefetch(self_in=self_in, self_out=self_out, cross_q=cross_q, cross_kv=cross_kv, cross_out=cross_out, own_t=own_t)
    step.near_out(
        triple_own=((half, 3 * width), bf16), self_bias=((length, length), f32), cross_bias=((length, length), f32)
    )
    (
        self_in_near, self_out_near, cross_q_near, cross_kv_near, cross_out_near, own_near, triple_own, self_bias, cross_bias,
    ) = step.run(first_body, 8 * macs, 12)

    step = Kernel(chain, place)
    step.near(other=other_t)
    step.near(self_in=self_in_near, self_out=self_out_near, own=own_near, triple_own=triple_own, bias=self_bias)
    step.far_out(triple=((length, 3 * width), bf16), mix=(square, bf16))
    step.heads_out(attn=(attn_shape, bf16))
    step.near_out(centre_first=(square, f32))
    triple, self_mix, self_attn, centre_first = step.run(self_forward_body, 24 * macs, 16)

    step = Kernel(chain, place)
    step.halves(memory=(own_m, other_m))
    step.near(centre_first=centre_first, cross_q=cross_q_near, cross_kv=cross_kv_near, cross_out=cross_out_near)
    step.near(vectors=vectors, bias=cross_bias)
    step.copy_out(centre_first_far=("centre_first", square, f32))
    step.far_out(query=(square, bf16), pairs=((length, 2 * width), bf16), mix=(square, bf16))
    step.heads_out(attn=(attn_shape, bf16))
    step.near_out(centre_second=(square, f32))
    step.prefetch(ffn_in=ffn_in, ffn_out=ffn_out)
    (
        centre_first, query, pairs, cross_mix, cross_attn, centre_second, ffn_in_near, ffn_out_near,
    ) = step.run(cross_forward_body, 24 * macs, 16)

    step = Kernel(chain, place)
    step.near(centre_second=centre_second, ffn_in=ffn_in_near, ffn_out=ffn_out_near, vectors=vectors)
    step.halves(cotangent=(own_c, other_c))
    step.far_out(output=((half, width), bf16))
    step.near_out(
        grad_second=(square, f32), sums=((8, width), f32), in_sums=((1, hidden), f32),
        keep=((rows, 2 * hidden), f32), send=((rows, 2 * hidden), bf16),
    )
    step.prefetch(cross_out=cross_out, query=query)
    step.hold(
        second=(square, bf16), active=((length, hidden), bf16), slope=((length, hidden), f32), outer=(square, bf16),
        inner=((length, hidden), bf16),
    )
    output, grad, sums, in_sums, feed_keep, feed_send, cross_out_near, query = step.run(feed_body, 40 * macs, 26)

    bits = lax.axis_size("wide").bit_length() - 1
    orders = {name: ORDER[name](bits) for name in ORDER}
    chunk_a = Chunk(chain, feed_keep, feed_send, orders["a"])
    chunks = dict(a=chunk_a)
    step = Kernel(chain, place)
    step.near(grad=grad, sums=sums, in_sums=in_sums, centre_second=centre_second, cross_out=cross_out_near, query=query)
    step.near(vectors=vectors)
    step.near_out(
        small=((16, half), f32), grad_second=(square, f32), grad_low=(square, bf16), dmix=(square, bf16),
        dmix_t=(square, bf16), query_t=(square, bf16),
    )
    step.prefetch(pairs=pairs, mix=cross_mix)
    step.hold(work=((8, width), f32))
    small, grad_second, grad_low, dmix, dmix_t, query_t, pairs, cross_mix = step.run(between_body, 24 * macs * 4, 8)
    for name in SCHEDULE[0]:
        chunks[name].advance()

    step = Kernel(chain, place)
    step.near(grad_second=grad_second, small=small, vectors=vectors, grad_low=grad_low, dmix=dmix, dmix_t=dmix_t)
    step.near(query_t=query_t, query=query, pairs=pairs, mix=cross_mix)
    step.heads("attn", cross_attn, 0, HEADS // 2)
    step.far(cross_kv=cross_kv)
    step.halves(memory=(own_m, other_m))
    step.far(centre_first=centre_first, cross_q=cross_q, self_mix=self_mix)
    step.far_out(memory_grad=((half, width), f32))
    step.near_out(
        grad_first=(square, f32), keep=((rows, 5 * width + 128), f32), send=((rows, 5 * width + 128), bf16)
    )
    step.prefetch(self_out=self_out, triple=triple, mix=self_mix)
    step.hold(
        first=(square, bf16), grad=(square, bf16), dquery=(square, bf16), dpairs_t=((2 * width, length), bf16), sums=((8, width), f32), turned=((128, half), f32),
    )
    memory_grad, grad_first, cross_keep, cross_send, self_out_near, triple, self_mix = step.run(cross_back_body, 48 * macs * 4, 24)

    chunk_c = chunks["c"] = Chunk(chain, cross_keep, cross_send, orders["c"])
    for name in SCHEDULE[1]:
        chunks[name].advance()

    def self_part(first, last):
        span = (last - first) * PAIR
        step = Kernel(chain, place)
        step.near(grad_first=grad_first)
        step.near(self_out=self_out_near, triple=triple, mix=self_mix)
        step.heads("attn", self_attn, first, last)
        step.halves(target=(own_t, other_t))
        step.far(self_in=self_in)
        step.far_out(target_grad=((half, width), f32))
        step.near_out(keep=((rows, 3 * span), f32), send=((rows, 3 * span), bf16))
        step.hold(
            grad=(square, bf16), dmix=((length, span), bf16), dmix_t=((span, length), bf16),
            query_t=((span, length), bf16), dquery=((length, span), bf16), dpairs_t=((2 * span, length), bf16),
        )
        return step.run(functools.partial(self_back_body, (first, last)), 24 * macs * 12, 16)

    target_grad, keep, send = self_part(0, HEADS // 2)
    chunk_d = chunks["d"] = Chunk(chain, keep, send, orders["d"])
    groups = hidden // width
    endings = dict(
        a=(
            [(0, group * half, 0, group * width, width) for group in range(groups)] + [(1, 0, 0, hidden, hidden)],
            [((groups * half, width), f32), ((half, hidden), f32)],
        ),
        c=(
            [(0, 0, 0, 0, width), (1, 0, 0, width, 2 * width), (2, 0, 0, 3 * width, width), (3, 0, 0, 4 * width, width)],
            [
                ((half, width), f32), ((half, 2 * width), f32), ((half, width), f32), ((half, width), f32),
                ((3, half), f32), ((3, half), f32), ((1, half), f32), ((1, groups * half), f32),
            ],
            [(4, 0, 0, 5), (4, 1, 0, 3), (4, 2, 0, 0), (5, 0, 0, 6), (5, 1, 0, 4), (5, 2, 0, 1), (6, 0, 0, 2)]
            + [(7, 0, row * half, 8 + row) for row in range(groups)],
        ),
        d=([(0, 0, 0, 0, 3 * width)], [((half, 3 * width), f32)]),
    )
    finished = {}
    for name in SCHEDULE[2]:
        if chunks[name].left():
            chunks[name].advance()
        elif name not in finished:
            finished[name] = chunks[name].finish(*endings[name])
    ffn_out_g, ffn_in_g = finished["a"]
    cross_q_g, cross_kv_g, cross_out_g, self_out_g, gain_g, shift_g, out_bias_g, in_bias_g = finished["c"]
    (self_in_g,) = finished["d"]
    return (
        output[None],
        target_grad[None],
        memory_grad[None],
        self_in_g,
        self_out_g,
        cross_q_g,
        cross_kv_g,
        cross_out_g,
        ffn_in_g,
        in_bias_g[0],
        ffn_out_g,
        out_bias_g[0],
        gain_g,
        shift_g,
    )


def fits_whole_rows(mesh, target, lens):
    wide, narrow = mesh.shape["wide"], mesh.shape["narrow"]
    rows, length, width = target.shape
    documents = lens.shape[1]
    return (
        narrow == 2
        and rows == wide
        and wide >= 2
        and wide & (wide - 1) == 0
        and length <= 512
        and documents == DOCUMENTS
        and width == HEADS * HEAD_DIM
        and width % (32 * wide) == 0
    )


def solution(mesh):
    in_specs = (
        P("wide", "narrow", None),
        P("wide", "narrow", None),
        P("wide", None),
        P("wide", None),
        P(),
        P(),
        P(),
        P(),
        P(),
        P(),
        P(),
        P(),
        P(),
        P(),
        P(),
        P("wide", "narrow", None),
    )
    out_specs = (
        P("wide", "narrow", None),
        P("wide", "narrow", None),
        P("wide", "narrow", None),
        P("narrow", None),
        P("narrow", None),
        P("narrow", None),
        P("narrow", None),
        P("narrow", None),
        P("narrow", None),
        P("narrow"),
        P("narrow", None),
        P("narrow"),
        P(None, "narrow"),
        P(None, "narrow"),
    )

    def layer(*arrays):
        body = whole_rows if fits_whole_rows(mesh, arrays[0], arrays[2]) else local
        return jax.shard_map(body, mesh=mesh, in_specs=in_specs, out_specs=out_specs, check_vma=False)(*arrays)

    return layer
```

profile of v0, /device:TPU:0, one launch (start us, length us, event | category | flops | bytes accessed | tf_op | source)
XLA Modules:
  0.0 119.3 jit_solution(12096857703504792332)
XLA Ops:
  0.6 3.0 %collective-permute-start.1 = (bf16[256,512]{1,0:T(8,128)(2,1)}, bf16[256,512]{1,0:T(8,128)(2,1)S(1)}, u32[]{:S(2)}, u32[]{:S(2)}) collective-permute-start(bf16[256,512]{1,0:T(8,128)(2,1)} %bitcast.14), channel_id=1, source_target_pairs={{0,1},{1,0},{2,3},{3,2},{4,5},{5,4},{6,7},{7,6},{8,9},{9,8},{10,11... | collective-permute-start | bytes 786440 | tf_op jit(solution)/shard_map/ppermute | solution.py:1115
  3.6 0.1 collective-permute-start
  3.7 1.9 %collective-permute-start.2 = (bf16[256,512]{1,0:T(8,128)(2,1)}, bf16[256,512]{1,0:T(8,128)(2,1)S(1)}, u32[]{:S(2)}, u32[]{:S(2)}) collective-permute-start(bf16[256,512]{1,0:T(8,128)(2,1)} %bitcast.21), channel_id=1, source_target_pairs={{0,1},{1,0},{2,3},{3,2},{4,5},{5,4},{6,7},{7,6},{8,9},{9,8},{10,11... | collective-permute-start | bytes 786440 | tf_op jit(solution)/shard_map/ppermute | solution.py:1115
  5.7 0.7 reshape.31
  6.4 0.8 concatenate.7
  7.1 0.8 concatenate.6.refs_0_
  7.9 3.5 %shard_map.263 = (bf16[512,1536]{1,0:T(8,128)(2,1)S(1)}, bf16[512,512]{1,0:T(8,128)(2,1)S(1)}, bf16[512,512]{1,0:T(8,128)(2,1)S(1)}, bf16[512,1024]{1,0:T(8,128)...) custom-call(s32[19]{0:T(128)S(1)} %concatenate.6.refs_0_, ...), custom_call_target="tpu_custom_call" | custom-call | flops 1073741824 | bytes 4718592 | tf_op jit(solution)/shard_map/pallas_call | solution.py:611
  11.4 7.0 %shard_map.264 = (bf16[512,1536]{1,0:T(8,128)(2,1)}, bf16[512,512]{1,0:T(8,128)(2,1)}, bf16[8,512,512]{2,1,0:T(8,128)(2,1)}, f32[512,512]{1,0:T(8,128)S(1)}, s32[8,128]{1,0:T(8,128)S(1)}) custom-call(s32[19]{0:T(128)S(1)} %concatenate.6.refs_0_, bf16[256,512]{1,0:T(8,128)(2,1)S(1)} %collective-permute-done.1.refs_1_.refs_7_, ...), custom_call_target="tpu_custom_call" | custom-call | flops 3221225472 | bytes 4460544 | tf_op jit(solution)/shard_map/pallas_call | solution.py:611
  18.5 0.0 collective-permute-done.refs_2_.refs_14_
  18.5 8.7 %shard_map.265 = (f32[512,512]{1,0:T(8,128)}, bf16[512,512]{1,0:T(8,128)(2,1)}, bf16[512,1024]{1,0:T(8,128)(2,1)}, bf16[512,512]{1,0:T(8,128)(2,1)}, bf16[8,512,...) custom-call(s32[19]{0:T(128)S(1)} %concatenate.6.refs_0_, ...), custom_call_target="tpu_custom_call" | custom-call | flops 3221225472 | bytes 8949760 | tf_op jit(solution)/shard_map/pallas_call | solution.py:611
  27.2 9.5 %shard_map.266 = (bf16[256,512]{1,0:T(8,128)(2,1)}, f32[512,512]{1,0:T(8,128)S(1)}, f32[8,512]{1,0:T(8,128)S(1)}, f32[1,2048]{1,0:T(1,128)S(1)}, f32[128,4096]{1...) custom-call(s32[19]{0:T(128)S(1)} %concatenate.6.refs_0_, ...), custom_call_target="tpu_custom_call" | custom-call | flops 5368709120 | bytes 6852608 | tf_op jit(solution)/shard_map/pallas_call | solution.py:611
  36.7 0.1 collective-permute-start.3
  36.8 3.1 %shard_map.267 = (f32[16,256]{1,0:T(8,128)S(1)}, f32[512,512]{1,0:T(8,128)S(1)}, bf16[512,512]{1,0:T(8,128)(2,1)S(1)}, bf16[512,512]{1,0:T(8,128)(2,1)S(1)}, bf1...) custom-call(s32[19]{0:T(128)S(1)} %concatenate.6.refs_0_, ...), custom_call_target="tpu_custom_call" | custom-call | flops 12884901888 | bytes 4780032 | tf_op jit(solution)/shard_map/pallas_call | solution.py:611
  39.9 0.4 shard_map.268
  40.3 1.7 %collective-permute-start.4 = (bf16[64,4096]{1,0:T(8,128)(2,1)S(1)}, bf16[64,4096]{1,0:T(8,128)(2,1)S(1)}, u32[]{:S(2)}, u32[]{:S(2)}) collective-permute-start(bf16[64,4096]{1,0:T(8,128)(2,1)S(1)} %get-tuple-element.172), channel_id=1, source_target_pairs={{0,4},{2,6},{4,0},{6,2},{8,12},{10,14},{12,8},{14,10},{16,20},{18,... | collective-permute-start | bytes 1572872 | tf_op jit(solution)/shard_map/ppermute | solution.py:963
  42.0 10.7 %shard_map.269 = (f32[256,512]{1,0:T(8,128)}, f32[512,512]{1,0:T(8,128)S(1)}, f32[128,2688]{1,0:T(8,128)S(1)}, bf16[128,2688]{1,0:T(8,128)(2,1)S(1)}, bf16[512,5...) custom-call(s32[19]{0:T(128)S(1)} %concatenate.6.refs_0_, ...), custom_call_target="tpu_custom_call" | custom-call | flops 25769803776 | bytes 15781888 | tf_op jit(solution)/shard_map/pallas_call | solution.py:611
  52.6 0.3 collective-permute-start.5
  52.9 1.7 %collective-permute-done.4.refs_1_ = bf16[64,4096]{1,0:T(8,128)(2,1)S(1)} collective-permute-done((bf16[64,4096]{1,0:T(8,128)(2,1)S(1)}, bf16[64,4096]{1,0:T(8,128)(2,1)S(1)}, u32[]{:S(2)}, u32[]{:S(2)}) %collective-permute-start.4) | collective-permute-done | bytes 524320 | tf_op jit(solution)/shard_map/ppermute | solution.py:963
  54.6 0.2 shard_map.270
  54.9 1.8 %collective-permute-start.6 = (bf16[32,4096]{1,0:T(8,128)(2,1)S(1)}, bf16[32,4096]{1,0:T(8,128)(2,1)S(1)}, u32[]{:S(2)}, u32[]{:S(2)}) collective-permute-start(bf16[32,4096]{1,0:T(8,128)(2,1)S(1)} %get-tuple-element.178), channel_id=1, source_target_pairs={{0,8},{2,10},{4,12},{6,14},{8,0},{10,2},{12,4},{14,6},{16,24},{18,... | collective-permute-start | bytes 786440 | tf_op jit(solution)/shard_map/ppermute | solution.py:963
  56.6 0.3 shard_map.271
  57.0 1.6 %collective-permute-start.7 = (bf16[64,2688]{1,0:T(8,128)(2,1)S(1)}, bf16[64,2688]{1,0:T(8,128)(2,1)S(1)}, u32[]{:S(2)}, u32[]{:S(2)}) collective-permute-start(bf16[64,2688]{1,0:T(8,128)(2,1)S(1)} %get-tuple-element.184), channel_id=1, source_target_pairs={{0,4},{2,6},{4,0},{6,2},{8,12},{10,14},{12,8},{14,10},{16,20},{18,... | collective-permute-start | bytes 1032200 | tf_op jit(solution)/shard_map/ppermute | solution.py:963
  58.5 4.3 %collective-permute-done.6.refs_1_ = bf16[32,4096]{1,0:T(8,128)(2,1)S(1)} collective-permute-done((bf16[32,4096]{1,0:T(8,128)(2,1)S(1)}, bf16[32,4096]{1,0:T(8,128)(2,1)S(1)}, u32[]{:S(2)}, u32[]{:S(2)}) %collective-permute-start.6) | collective-permute-done | bytes 262176 | tf_op jit(solution)/shard_map/ppermute | solution.py:963
  62.9 0.1 shard_map.272
  62.9 2.8 %collective-permute-start.8 = (bf16[32,4096]{1,0:T(8,128)(2,1)S(1)}, bf16[32,4096]{1,0:T(8,128)(2,1)S(1)}, u32[]{:S(2)}, u32[]{:S(2)}) collective-permute-start(bf16[32,4096]{1,0:T(8,128)(2,1)S(1)} %get-tuple-element.186.refs_0_), channel_id=1, source_target_pairs={{0,16},{2,18},{4,20},{6,22},{8,24},{10,26},{12,28},{14,30},{16,0},... | collective-permute-start | bytes 786440 | tf_op jit(solution)/shard_map/ppermute | solution.py:963
  65.7 7.7 %shard_map.273 = (f32[256,512]{1,0:T(8,128)}, f32[128,1536]{1,0:T(8,128)S(1)}, bf16[128,1536]{1,0:T(8,128)(2,1)S(1)}, s32[8,128]{1,0:T(8,128)S(1)}) custom-call(s32[19]{0:T(128)S(1)} %concatenate.6.refs_0_, f32[512,512]{1,0:T(8,128)S(1)} %get-tuple-element.165.refs_1_, bf16[512,512]{1,0:T(8,128)(2,1)S(1)} %get-tuple-element.166.refs_2_, ...), custom_call_target="tpu_custom_call" | custom-call | flops 38654705664 | bytes 9965568 | tf_op jit(solution)/shard_map/pallas_call | solution.py:611
  73.4 0.1 collective-permute-start.9
  73.5 0.2 shard_map.274
  73.7 1.7 %collective-permute-start.10 = (bf16[32,2688]{1,0:T(8,128)(2,1)S(1)}, bf16[32,2688]{1,0:T(8,128)(2,1)S(1)}, u32[]{:S(2)}, u32[]{:S(2)}) collective-permute-start(bf16[32,2688]{1,0:T(8,128)(2,1)S(1)} %get-tuple-element.192), channel_id=1, source_target_pairs={{0,8},{2,10},{4,12},{6,14},{8,0},{10,2},{12,4},{14,6},{16,24},{18,... | collective-permute-start | bytes 516104 | tf_op jit(solution)/shard_map/ppermute | solution.py:963
  75.3 1.3 %collective-permute-done.8.refs_1_ = bf16[32,4096]{1,0:T(8,128)(2,1)S(1)} collective-permute-done((bf16[32,4096]{1,0:T(8,128)(2,1)S(1)}, bf16[32,4096]{1,0:T(8,128)(2,1)S(1)}, u32[]{:S(2)}, u32[]{:S(2)}) %collective-permute-start.8) | collective-permute-done | bytes 262176 | tf_op jit(solution)/shard_map/ppermute | solution.py:963
  76.6 0.1 shard_map.275
  76.7 0.8 collective-permute-start.11
  77.5 0.2 shard_map.276
  77.7 1.6 %collective-permute-start.12 = (bf16[64,1536]{1,0:T(8,128)(2,1)S(1)}, bf16[64,1536]{1,0:T(8,128)(2,1)S(1)}, u32[]{:S(2)}, u32[]{:S(2)}) collective-permute-start(bf16[64,1536]{1,0:T(8,128)(2,1)S(1)} %get-tuple-element.197), channel_id=1, source_target_pairs={{0,4},{2,6},{4,0},{6,2},{8,12},{10,14},{12,8},{14,10},{16,20},{18,... | collective-permute-start | bytes 589832 | tf_op jit(solution)/shard_map/ppermute | solution.py:963
  79.3 1.6 %collective-permute-done.10.refs_1_ = bf16[32,2688]{1,0:T(8,128)(2,1)S(1)} collective-permute-done((bf16[32,2688]{1,0:T(8,128)(2,1)S(1)}, bf16[32,2688]{1,0:T(8,128)(2,1)S(1)}, u32[]{:S(2)}, u32[]{:S(2)}) %collective-permute-start.10) | collective-permute-done | bytes 172064 | tf_op jit(solution)/shard_map/ppermute | solution.py:963
  81.0 1.9 %collective-permute-start.13 = (bf16[32,2688]{1,0:T(8,128)(2,1)S(1)}, bf16[32,2688]{1,0:T(8,128)(2,1)S(1)}, u32[]{:S(2)}, u32[]{:S(2)}) collective-permute-start(bf16[32,2688]{1,0:T(8,128)(2,1)S(1)} %get-tuple-element.199.refs_0_), channel_id=1, source_target_pairs={{0,16},{2,18},{4,20},{6,22},{8,24},{10,26},{12,28},{14,30},{16,0},... | collective-permute-start | bytes 516104 | tf_op jit(solution)/shard_map/ppermute | solution.py:963
  82.9 6.3 %collective-permute-done.11.refs_1_ = bf16[32,4096]{1,0:T(8,128)(2,1)S(1)} collective-permute-done((bf16[32,4096]{1,0:T(8,128)(2,1)S(1)}, bf16[32,4096]{1,0:T(8,128)(2,1)S(1)}, u32[]{:S(2)}, u32[]{:S(2)}) %collective-permute-start.11) | collective-permute-done | bytes 262176 | tf_op jit(solution)/shard_map/ppermute | solution.py:963
  89.2 0.1 shard_map.278
  89.3 1.6 %collective-permute-start.17 = (bf16[64,4096]{1,0:T(8,128)(2,1)S(1)}, bf16[64,4096]{1,0:T(8,128)(2,1)S(1)}, u32[]{:S(2)}, u32[]{:S(2)}) collective-permute-start(bf16[64,4096]{1,0:T(8,128)(2,1)S(1)} %get-tuple-element.208.refs_0_), channel_id=1, source_target_pairs={{0,4},{2,6},{4,0},{6,2},{8,12},{10,14},{12,8},{14,10},{16,20},{18,... | collective-permute-start | bytes 1572872 | tf_op jit(solution)/shard_map/ppermute | solution.py:963
  90.9 0.1 shard_map.279
  91.1 0.1 collective-permute-start.14
  91.2 0.1 collective-permute-done.13.refs_1_
  91.3 2.0 %collective-permute-start.15 = (bf16[32,2688]{1,0:T(8,128)(2,1)S(1)}, bf16[32,2688]{1,0:T(8,128)(2,1)S(1)}, u32[]{:S(2)}, u32[]{:S(2)}) collective-permute-start(bf16[32,2688]{1,0:T(8,128)(2,1)S(1)} %get-tuple-element.204.refs_0_), channel_id=1, source_target_pairs={{0,8},{2,10},{4,12},{6,14},{8,0},{10,2},{12,4},{14,6},{16,24},{18,... | collective-permute-start | bytes 516104 | tf_op jit(solution)/shard_map/ppermute | solution.py:963
  93.3 3.6 %collective-permute-done.14.refs_1_ = bf16[32,1536]{1,0:T(8,128)(2,1)S(1)} collective-permute-done((bf16[32,1536]{1,0:T(8,128)(2,1)S(1)}, bf16[32,1536]{1,0:T(8,128)(2,1)S(1)}, u32[]{:S(2)}, u32[]{:S(2)}) %collective-permute-start.14) | collective-permute-done | bytes 98336 | tf_op jit(solution)/shard_map/ppermute | solution.py:963
  96.9 0.4 collective-permute-start.16
  97.3 2.7 %collective-permute-done.15.refs_1_ = bf16[32,2688]{1,0:T(8,128)(2,1)S(1)} collective-permute-done((bf16[32,2688]{1,0:T(8,128)(2,1)S(1)}, bf16[32,2688]{1,0:T(8,128)(2,1)S(1)}, u32[]{:S(2)}, u32[]{:S(2)}) %collective-permute-start.15) | collective-permute-done | bytes 172064 | tf_op jit(solution)/shard_map/ppermute | solution.py:963
  100.0 0.1 shard_map.282
  100.2 0.6 collective-permute-start.19
  100.7 2.3 %collective-permute-done.16.refs_1_ = bf16[32,1536]{1,0:T(8,128)(2,1)S(1)} collective-permute-done((bf16[32,1536]{1,0:T(8,128)(2,1)S(1)}, bf16[32,1536]{1,0:T(8,128)(2,1)S(1)}, u32[]{:S(2)}, u32[]{:S(2)}) %collective-permute-start.16) | collective-permute-done | bytes 98336 | tf_op jit(solution)/shard_map/ppermute | solution.py:963
  103.1 0.1 collective-permute-start.18
  103.1 1.1 collective-permute-done.17.refs_1_
  104.2 0.2 shard_map.284
  104.4 3.3 %collective-permute-done.18.refs_1_ = bf16[32,1536]{1,0:T(8,128)(2,1)S(1)} collective-permute-done((bf16[32,1536]{1,0:T(8,128)(2,1)S(1)}, bf16[32,1536]{1,0:T(8,128)(2,1)S(1)}, u32[]{:S(2)}, u32[]{:S(2)}) %collective-permute-start.18) | collective-permute-done | bytes 98336 | tf_op jit(solution)/shard_map/ppermute | solution.py:963
  107.7 0.1 shard_map.285
  107.9 0.6 collective-permute-start.22
  108.4 3.1 %collective-permute-done.19.refs_1_ = bf16[64,2688]{1,0:T(8,128)(2,1)S(1)} collective-permute-done((bf16[64,2688]{1,0:T(8,128)(2,1)S(1)}, bf16[64,2688]{1,0:T(8,128)(2,1)S(1)}, u32[]{:S(2)}, u32[]{:S(2)}) %collective-permute-start.19) | collective-permute-done | bytes 344096 | tf_op jit(solution)/shard_map/ppermute | solution.py:963
  111.6 0.2 shard_map.286
  111.7 0.1 collective-permute-start.21
  111.8 2.3 %shard_map.287 = (f32[1024,512]{1,0:T(8,128)}, f32[256,2048]{1,0:T(8,128)}, s32[8,128]{1,0:T(8,128)S(1)}) custom-call(s32[8,128]{1,0:T(8,128)S(1)} %get-tuple-element.213.token_ref, bf16[128,4096]{1,0:T(8,128)(2,1)S(1)} %get-tuple-element.214.refs_0_, bf16[128,4096]{1,0:T(8,128)(2,1)S(1)} %collective-permute-done.20.refs_1_), custom_call_target="tpu_custom_call" | custom-call | flops 24999999488 | bytes 1 | tf_op jit(solution)/shard_map/pallas_call | solution.py:978
  114.2 1.7 %shard_map.288 = (f32[256,512]{1,0:T(8,128)}, f32[256,1024]{1,0:T(8,128)}, f32[256,512]{1,0:T(8,128)}, f32[256,512]{1,0:T(8,128)}, f32[3,256]{1,0:T(4,128)}, /*i...) custom-call(s32[8,128]{1,0:T(8,128)S(1)} %get-tuple-element.215.token_ref, ...), custom_call_target="tpu_custom_call" | custom-call | flops 24999999488 | bytes 1 | tf_op jit(solution)/shard_map/pallas_call | solution.py:978
  115.9 0.1 shard_map.289
  116.0 0.6 collective-permute-start.23
  116.6 1.3 %collective-permute-done.23.refs_1_ = bf16[128,1536]{1,0:T(8,128)(2,1)S(1)} collective-permute-done((bf16[128,1536]{1,0:T(8,128)(2,1)S(1)}, bf16[128,1536]{1,0:T(8,128)(2,1)S(1)}, u32[]{:S(2)}, u32[]{:S(2)}) %collective-permute-start.23) | collective-permute-done | bytes 393248 | tf_op jit(solution)/shard_map/ppermute | solution.py:963
  117.9 1.3 %shard_map.290 = (f32[256,1536]{1,0:T(8,128)}, s32[8,128]{1,0:T(8,128)}) custom-call(s32[8,128]{1,0:T(8,128)S(1)} %get-tuple-element.219.token_ref, bf16[128,1536]{1,0:T(8,128)(2,1)S(1)} %get-tuple-element.220.refs_0_, bf16[128,1536]{1,0:T(8,128)(2,1)S(1)} %collective-permute-done.23.refs_1_), custom_call_target="tpu_custom_call" | custom-call | flops 24999999488 | bytes 1 | tf_op jit(solution)/shard_map/pallas_call | solution.py:978
  (17 shorter events, 0.2 us)
Async XLA Ops:
  0.6 10.8 %collective-permute-start.1 = (bf16[256,512]{1,0:T(8,128)(2,1)}, bf16[256,512]{1,0:T(8,128)(2,1)S(1)}, u32[]{:S(2)}, u32[]{:S(2)}) collective-permute-start(bf16[256,512]{1,0:T(8,128)(2,1)} %bitcast.14), channel_id=1, source_target_pairs={{0,1},{1,0},{2,3},{3,2},{4,5},{5,4},{6,7},{7,6},{8,9},{9,8},{10,11... | collective-permute-start | bytes 786440 | tf_op jit(solution)/shard_map/ppermute | solution.py:1115
  3.6 14.8 %collective-permute-start = (bf16[256,512]{1,0:T(8,128)(2,1)}, bf16[256,512]{1,0:T(8,128)(2,1)S(1)}, u32[]{:S(2)}, u32[]{:S(2)}) collective-permute-start(bf16[256,512]{1,0:T(8,128)(2,1)} %bitcast.23), channel_id=1, source_target_pairs={{0,1},{1,0},{2,3},{3,2},{4,5},{5,4},{6,7},{7,6},{8,9},{9,8},{10,11... | collective-permute-start | bytes 786440 | tf_op jit(solution)/shard_map/ppermute | solution.py:1115
  3.7 23.5 %collective-permute-start.2 = (bf16[256,512]{1,0:T(8,128)(2,1)}, bf16[256,512]{1,0:T(8,128)(2,1)S(1)}, u32[]{:S(2)}, u32[]{:S(2)}) collective-permute-start(bf16[256,512]{1,0:T(8,128)(2,1)} %bitcast.21), channel_id=1, source_target_pairs={{0,1},{1,0},{2,3},{3,2},{4,5},{5,4},{6,7},{7,6},{8,9},{9,8},{10,11... | collective-permute-start | bytes 786440 | tf_op jit(solution)/shard_map/ppermute | solution.py:1115
  36.7 3.2 %collective-permute-start.3 = (bf16[128,4096]{1,0:T(8,128)(2,1)S(1)}, bf16[128,4096]{1,0:T(8,128)(2,1)S(1)}, u32[]{:S(2)}, u32[]{:S(2)}) collective-permute-start(bf16[128,4096]{1,0:T(8,128)(2,1)S(1)} %get-tuple-element.163), channel_id=1, source_target_pairs={{0,2},{2,0},{4,6},{6,4},{8,10},{10,8},{12,14},{14,12},{16,18},{18,... | collective-permute-start | bytes 3145736 | tf_op jit(solution)/shard_map/ppermute | solution.py:963
  40.3 14.4 %collective-permute-start.4 = (bf16[64,4096]{1,0:T(8,128)(2,1)S(1)}, bf16[64,4096]{1,0:T(8,128)(2,1)S(1)}, u32[]{:S(2)}, u32[]{:S(2)}) collective-permute-start(bf16[64,4096]{1,0:T(8,128)(2,1)S(1)} %get-tuple-element.172), channel_id=1, source_target_pairs={{0,4},{2,6},{4,0},{6,2},{8,12},{10,14},{12,8},{14,10},{16,20},{18,... | collective-permute-start | bytes 1572872 | tf_op jit(solution)/shard_map/ppermute | solution.py:963
  52.6 4.0 %collective-permute-start.5 = (bf16[128,2688]{1,0:T(8,128)(2,1)S(1)}, bf16[128,2688]{1,0:T(8,128)(2,1)S(1)}, u32[]{:S(2)}, u32[]{:S(2)}) collective-permute-start(bf16[128,2688]{1,0:T(8,128)(2,1)S(1)} %get-tuple-element.175), channel_id=1, source_target_pairs={{0,2},{2,0},{4,6},{6,4},{8,10},{10,8},{12,14},{14,12},{16,18},{18,... | collective-permute-start | bytes 2064392 | tf_op jit(solution)/shard_map/ppermute | solution.py:963
  54.9 8.0 %collective-permute-start.6 = (bf16[32,4096]{1,0:T(8,128)(2,1)S(1)}, bf16[32,4096]{1,0:T(8,128)(2,1)S(1)}, u32[]{:S(2)}, u32[]{:S(2)}) collective-permute-start(bf16[32,4096]{1,0:T(8,128)(2,1)S(1)} %get-tuple-element.178), channel_id=1, source_target_pairs={{0,8},{2,10},{4,12},{6,14},{8,0},{10,2},{12,4},{14,6},{16,24},{18,... | collective-permute-start | bytes 786440 | tf_op jit(solution)/shard_map/ppermute | solution.py:963
  57.0 16.5 %collective-permute-start.7 = (bf16[64,2688]{1,0:T(8,128)(2,1)S(1)}, bf16[64,2688]{1,0:T(8,128)(2,1)S(1)}, u32[]{:S(2)}, u32[]{:S(2)}) collective-permute-start(bf16[64,2688]{1,0:T(8,128)(2,1)S(1)} %get-tuple-element.184), channel_id=1, source_target_pairs={{0,4},{2,6},{4,0},{6,2},{8,12},{10,14},{12,8},{14,10},{16,20},{18,... | collective-permute-start | bytes 1032200 | tf_op jit(solution)/shard_map/ppermute | solution.py:963
  62.9 13.7 %collective-permute-start.8 = (bf16[32,4096]{1,0:T(8,128)(2,1)S(1)}, bf16[32,4096]{1,0:T(8,128)(2,1)S(1)}, u32[]{:S(2)}, u32[]{:S(2)}) collective-permute-start(bf16[32,4096]{1,0:T(8,128)(2,1)S(1)} %get-tuple-element.186.refs_0_), channel_id=1, source_target_pairs={{0,16},{2,18},{4,20},{6,22},{8,24},{10,26},{12,28},{14,30},{16,0},... | collective-permute-start | bytes 786440 | tf_op jit(solution)/shard_map/ppermute | solution.py:963
  73.4 4.1 %collective-permute-start.9 = (bf16[128,1536]{1,0:T(8,128)(2,1)S(1)}, bf16[128,1536]{1,0:T(8,128)(2,1)S(1)}, u32[]{:S(2)}, u32[]{:S(2)}) collective-permute-start(bf16[128,1536]{1,0:T(8,128)(2,1)S(1)} %get-tuple-element.189), channel_id=1, source_target_pairs={{0,2},{2,0},{4,6},{6,4},{8,10},{10,8},{12,14},{14,12},{16,18},{18,... | collective-permute-start | bytes 1179656 | tf_op jit(solution)/shard_map/ppermute | solution.py:963
  73.7 7.2 %collective-permute-start.10 = (bf16[32,2688]{1,0:T(8,128)(2,1)S(1)}, bf16[32,2688]{1,0:T(8,128)(2,1)S(1)}, u32[]{:S(2)}, u32[]{:S(2)}) collective-permute-start(bf16[32,2688]{1,0:T(8,128)(2,1)S(1)} %get-tuple-element.192), channel_id=1, source_target_pairs={{0,8},{2,10},{4,12},{6,14},{8,0},{10,2},{12,4},{14,6},{16,24},{18,... | collective-permute-start | bytes 516104 | tf_op jit(solution)/shard_map/ppermute | solution.py:963
  76.7 12.5 %collective-permute-start.11 = (bf16[32,4096]{1,0:T(8,128)(2,1)S(1)}, bf16[32,4096]{1,0:T(8,128)(2,1)S(1)}, u32[]{:S(2)}, u32[]{:S(2)}) collective-permute-start(bf16[32,4096]{1,0:T(8,128)(2,1)S(1)} %get-tuple-element.194.refs_0_), channel_id=1, source_target_pairs={{0,8},{2,10},{4,12},{6,14},{8,0},{10,2},{12,4},{14,6},{16,24},{18,... | collective-permute-start | bytes 786440 | tf_op jit(solution)/shard_map/ppermute | solution.py:963
  77.7 13.2 %collective-permute-start.12 = (bf16[64,1536]{1,0:T(8,128)(2,1)S(1)}, bf16[64,1536]{1,0:T(8,128)(2,1)S(1)}, u32[]{:S(2)}, u32[]{:S(2)}) collective-permute-start(bf16[64,1536]{1,0:T(8,128)(2,1)S(1)} %get-tuple-element.197), channel_id=1, source_target_pairs={{0,4},{2,6},{4,0},{6,2},{8,12},{10,14},{12,8},{14,10},{16,20},{18,... | collective-permute-start | bytes 589832 | tf_op jit(solution)/shard_map/ppermute | solution.py:963
  81.0 10.3 %collective-permute-start.13 = (bf16[32,2688]{1,0:T(8,128)(2,1)S(1)}, bf16[32,2688]{1,0:T(8,128)(2,1)S(1)}, u32[]{:S(2)}, u32[]{:S(2)}) collective-permute-start(bf16[32,2688]{1,0:T(8,128)(2,1)S(1)} %get-tuple-element.199.refs_0_), channel_id=1, source_target_pairs={{0,16},{2,18},{4,20},{6,22},{8,24},{10,26},{12,28},{14,30},{16,0},... | collective-permute-start | bytes 516104 | tf_op jit(solution)/shard_map/ppermute | solution.py:963
  89.3 14.9 %collective-permute-start.17 = (bf16[64,4096]{1,0:T(8,128)(2,1)S(1)}, bf16[64,4096]{1,0:T(8,128)(2,1)S(1)}, u32[]{:S(2)}, u32[]{:S(2)}) collective-permute-start(bf16[64,4096]{1,0:T(8,128)(2,1)S(1)} %get-tuple-element.208.refs_0_), channel_id=1, source_target_pairs={{0,4},{2,6},{4,0},{6,2},{8,12},{10,14},{12,8},{14,10},{16,20},{18,... | collective-permute-start | bytes 1572872 | tf_op jit(solution)/shard_map/ppermute | solution.py:963
  91.1 5.8 %collective-permute-start.14 = (bf16[32,1536]{1,0:T(8,128)(2,1)S(1)}, bf16[32,1536]{1,0:T(8,128)(2,1)S(1)}, u32[]{:S(2)}, u32[]{:S(2)}) collective-permute-start(bf16[32,1536]{1,0:T(8,128)(2,1)S(1)} %get-tuple-element.202), channel_id=1, source_target_pairs={{0,8},{2,10},{4,12},{6,14},{8,0},{10,2},{12,4},{14,6},{16,24},{18,... | collective-permute-start | bytes 294920 | tf_op jit(solution)/shard_map/ppermute | solution.py:963
  91.3 8.7 %collective-permute-start.15 = (bf16[32,2688]{1,0:T(8,128)(2,1)S(1)}, bf16[32,2688]{1,0:T(8,128)(2,1)S(1)}, u32[]{:S(2)}, u32[]{:S(2)}) collective-permute-start(bf16[32,2688]{1,0:T(8,128)(2,1)S(1)} %get-tuple-element.204.refs_0_), channel_id=1, source_target_pairs={{0,8},{2,10},{4,12},{6,14},{8,0},{10,2},{12,4},{14,6},{16,24},{18,... | collective-permute-start | bytes 516104 | tf_op jit(solution)/shard_map/ppermute | solution.py:963
  96.9 6.1 %collective-permute-start.16 = (bf16[32,1536]{1,0:T(8,128)(2,1)S(1)}, bf16[32,1536]{1,0:T(8,128)(2,1)S(1)}, u32[]{:S(2)}, u32[]{:S(2)}) collective-permute-start(bf16[32,1536]{1,0:T(8,128)(2,1)S(1)} %get-tuple-element.206.refs_0_), channel_id=1, source_target_pairs={{0,16},{2,18},{4,20},{6,22},{8,24},{10,26},{12,28},{14,30},{16,0},... | collective-permute-start | bytes 294920 | tf_op jit(solution)/shard_map/ppermute | solution.py:963
  100.2 11.4 %collective-permute-start.19 = (bf16[64,2688]{1,0:T(8,128)(2,1)S(1)}, bf16[64,2688]{1,0:T(8,128)(2,1)S(1)}, u32[]{:S(2)}, u32[]{:S(2)}) collective-permute-start(bf16[64,2688]{1,0:T(8,128)(2,1)S(1)} %get-tuple-element.212.refs_0_), channel_id=1, source_target_pairs={{0,4},{2,6},{4,0},{6,2},{8,12},{10,14},{12,8},{14,10},{16,20},{18,... | collective-permute-start | bytes 1032200 | tf_op jit(solution)/shard_map/ppermute | solution.py:963
  103.1 4.7 %collective-permute-start.18 = (bf16[32,1536]{1,0:T(8,128)(2,1)S(1)}, bf16[32,1536]{1,0:T(8,128)(2,1)S(1)}, u32[]{:S(2)}, u32[]{:S(2)}) collective-permute-start(bf16[32,1536]{1,0:T(8,128)(2,1)S(1)} %get-tuple-element.210.refs_0_), channel_id=1, source_target_pairs={{0,8},{2,10},{4,12},{6,14},{8,0},{10,2},{12,4},{14,6},{16,24},{18,... | collective-permute-start | bytes 294920 | tf_op jit(solution)/shard_map/ppermute | solution.py:963
  107.9 8.0 %collective-permute-start.22 = (bf16[64,1536]{1,0:T(8,128)(2,1)S(1)}, bf16[64,1536]{1,0:T(8,128)(2,1)S(1)}, u32[]{:S(2)}, u32[]{:S(2)}) collective-permute-start(bf16[64,1536]{1,0:T(8,128)(2,1)S(1)} %get-tuple-element.218.refs_0_), channel_id=1, source_target_pairs={{0,4},{2,6},{4,0},{6,2},{8,12},{10,14},{12,8},{14,10},{16,20},{18,... | collective-permute-start | bytes 589832 | tf_op jit(solution)/shard_map/ppermute | solution.py:963
  108.4 3.4 %collective-permute-start.20 = (bf16[128,4096]{1,0:T(8,128)(2,1)S(1)}, bf16[128,4096]{1,0:T(8,128)(2,1)S(1)}, u32[]{:S(2)}, u32[]{:S(2)}) collective-permute-start(bf16[128,4096]{1,0:T(8,128)(2,1)S(1)} %get-tuple-element.214.refs_0_), channel_id=1, source_target_pairs={{0,2},{2,0},{4,6},{6,4},{8,10},{10,8},{12,14},{14,12},{16,18},{18,... | collective-permute-start | bytes 3145736 | tf_op jit(solution)/shard_map/ppermute | solution.py:963
  111.7 2.4 %collective-permute-start.21 = (bf16[128,2688]{1,0:T(8,128)(2,1)S(1)}, bf16[128,2688]{1,0:T(8,128)(2,1)S(1)}, u32[]{:S(2)}, u32[]{:S(2)}) collective-permute-start(bf16[128,2688]{1,0:T(8,128)(2,1)S(1)} %get-tuple-element.216.refs_0_), channel_id=1, source_target_pairs={{0,2},{2,0},{4,6},{6,4},{8,10},{10,8},{12,14},{14,12},{16,18},{18,... | collective-permute-start | bytes 2064392 | tf_op jit(solution)/shard_map/ppermute | solution.py:963
  116.0 1.9 %collective-permute-start.23 = (bf16[128,1536]{1,0:T(8,128)(2,1)S(1)}, bf16[128,1536]{1,0:T(8,128)(2,1)S(1)}, u32[]{:S(2)}, u32[]{:S(2)}) collective-permute-start(bf16[128,1536]{1,0:T(8,128)(2,1)S(1)} %get-tuple-element.220.refs_0_), channel_id=1, source_target_pairs={{0,2},{2,0},{4,6},{6,4},{8,10},{10,8},{12,14},{14,12},{16,18},{18,... | collective-permute-start | bytes 1179656 | tf_op jit(solution)/shard_map/ppermute | solution.py:963
where the time goes:
time: 120 us; the launch traced here: 119 us
  Pallas kernels  58.1 us (48%)
  waiting for transfers between devices  32.9 us (27%)
  starting transfers between devices  25.1 us (21%)
  local copies, waits for them, and re-layouts  2.22 us (2%)
    pallas_call x7, Pallas kernels, run(): pl.pallas_call(kernel, out_shape=shapes, in_specs=[pl.BlockSpec(memory_sp...  50.2 us
    ppermute x21, waiting for transfers between devices, send_wide(): lax.ppermute(values, 'wide', [(i, i ^ 1 << bit) for i in range(count)])  32.9 us
    ppermute x21, starting transfers between devices, send_wide(): lax.ppermute(values, 'wide', [(i, i ^ 1 << bit) for i in range(count)])  20.1 us
    pallas_call x21, Pallas kernels, small_kernel(): pl.pallas_call(kernel, out_shape=[jax.ShapeDtypeStruct(shape, dtype) for...  7.97 us
    ppermute x3, starting transfers between devices, other_half(): return lax.ppermute(values, 'narrow', [(0, 1), (1, 0)])  5.03 us
  transfers between devices with their start and end apart: 24, of which 13 were waited for; matrix products, arithmetic and copies ran while one was open for 2% of the time, Pallas kernels for 39%

commit v1 on v0

--- a/solution.py
+++ b/solution.py
@@ -658,30 +658,66 @@
     return (lane < HEAD_DIM, lane >= HEAD_DIM)
 
 
-def attend_all(query_ref, key_ref, value_ref, bias_ref, attn, mix_ref, causal):
+SPAN = 32
+
+
+def attend_all(query_ref, key_ref, value_ref, bias_ref, attn, mix_ref, work_ref, causal):
     length = query_ref.shape[0]
 
     def one_pair(pair, carry):
         lanes = pl.ds(pl.multiple_of(pair * PAIR, PAIR), PAIR)
         keys, values = key_ref[:, lanes], value_ref[:, lanes]
         zero = jnp.zeros_like(keys)
-        for begin, end, reach in query_blocks(length, causal):
-            queries = query_ref[begin:end, lanes]
-            total = jnp.zeros((end - begin, PAIR), jnp.float32)
-            for sub, inside in enumerate(head_lanes()):
-                scores = dot_nt(queries, jnp.where(inside, keys, zero)[:reach])
-                scores = scores + bias_ref[begin:end, :reach]
+        total = jnp.zeros((length, PAIR), jnp.float32)
+        for sub, inside in enumerate(head_lanes()):
+            work_ref[sub] = dot_nt(query_ref[:, lanes], jnp.where(inside, keys, zero))
+            for begin in range(0, length, SPAN):
+                rows = slice(begin, begin + SPAN)
+                reach = length // 2 if causal and begin + SPAN <= length // 2 else length
+                scores = work_ref[sub, rows, :reach] + bias_ref[rows, :reach]
                 weights = jnp.exp(scores - jnp.max(scores, axis=-1, keepdims=True))
                 weights = low(weights * (1.0 / jnp.sum(weights, axis=-1, keepdims=True)))
-                attn.near[pair * 2 + sub, begin:end, :reach] = weights
+                attn.near[pair * 2 + sub, rows, :reach] = weights
                 if reach < length:
-                    attn.near[pair * 2 + sub, begin:end, reach:] = jnp.zeros((end - begin, length - reach), weights.dtype)
-                total = total + dot_nn(weights, jnp.where(inside, values, zero)[:reach])
-            mix_ref[begin:end, lanes] = low(total)
+                    attn.near[pair * 2 + sub, rows, reach:] = jnp.zeros((SPAN, length - reach), weights.dtype)
+            total = total + dot_nn(attn.near[pair * 2 + sub], jnp.where(inside, values, zero))
+        mix_ref[:, lanes] = low(total)
         attn.copy(pair).start()
         return carry
 
     lax.fori_loop(0, HEADS // 2, one_pair, 0, unroll=True)
+
+
+def attend_whole_back(
+    query_ref, query_t_ref, key_ref, value_ref, attn, mix_ref, grad_ref, grad_t_ref, dquery_ref, dpairs_t_ref,
+    work_ref, dscores_ref,
+):
+    length, width = query_ref.shape
+
+    def one_pair(pair, carry):
+        lanes = pl.ds(pl.multiple_of(pair * PAIR, PAIR), PAIR)
+        attn.copy(pair).wait()
+        keys, values = key_ref[:, lanes], value_ref[:, lanes]
+        zero = jnp.zeros_like(keys)
+        dquery = jnp.zeros((length, PAIR), jnp.float32)
+        dots = grad_ref[:, lanes].astype(jnp.float32) * mix_ref[:, lanes].astype(jnp.float32)
+        for sub, inside in enumerate(head_lanes()):
+            row_dot = jnp.sum(jnp.where(inside, dots, 0.0), axis=-1, keepdims=True)
+            work_ref[sub] = dot_nt(grad_ref[:, lanes], jnp.where(inside, values, zero))
+            for begin in range(0, length, SPAN):
+                rows = slice(begin, begin + SPAN)
+                weights = attn.near[pair * 2 + sub, rows, :].astype(jnp.float32)
+                dscores_ref[sub, rows, :] = low(weights * (work_ref[sub, rows, :] - row_dot[rows]))
+            dquery = dquery + dot_nn(dscores_ref[sub], jnp.where(inside, keys, zero))
+            first = pair * PAIR + sub * HEAD_DIM
+            rows = pl.ds(pl.multiple_of(first, HEAD_DIM), HEAD_DIM)
+            dpairs_t_ref[rows, :] = low(dot_nn(query_t_ref[rows, :], dscores_ref[sub]))
+            where = pl.ds(pl.multiple_of(width + first, HEAD_DIM), HEAD_DIM)
+            dpairs_t_ref[where, :] = low(dot_nn(grad_t_ref[rows, :], attn.near[pair * 2 + sub]))
+        dquery_ref[:, lanes] = low(dquery * HEAD_DIM ** (-0.5))
+        return carry
+
+    lax.fori_loop(0, HEADS // 2, one_pair, 0)
 
 
 def attend_all_back(
@@ -765,7 +801,7 @@
     triple.start()
     attend_all(
         triple.near.at[:, :width], triple.near.at[:, width : 2 * width], triple.near.at[:, 2 * width :],
-        views.bias, views.attn, mix.near, True,
+        views.bias, views.attn, mix.near, views.work, True,
     )
     mix.start()
     centre_ref = views.centre_first
@@ -784,7 +820,9 @@
     query.start()
     pairs.near[...] = low(dot_nn(views.memory.get()[...], views.cross_kv[...]))
     pairs.start()
-    attend_all(query.near, pairs.near.at[:, :width], pairs.near.at[:, width:], bias_ref, views.attn, mix.near, False)
+    attend_all(
+        query.near, pairs.near.at[:, :width], pairs.near.at[:, width:], bias_ref, views.attn, mix.near, views.work, False
+    )
     mix.start()
     first = unit_of(centre_first_ref[...])[0] * gain_of(vectors_ref, 0) + shift_of(vectors_ref, 0)
     views.centre_second[...] = centred(first + dot_nn(mix.near[...], views.cross_out[...]))
@@ -891,9 +929,9 @@
     grad_second_ref = views.grad_second
     query_ref = views.query
     pairs_ref, mix_ref = views.pairs, views.mix
-    attend_all_back(
-        (0, HEADS // 2), query_ref, query_t_ref, pairs_ref.at[:, :width], pairs_ref.at[:, width:], views.attn, mix_ref,
-        dmix_ref, dmix_t_ref, dquery_ref, dpairs_t_ref, False,
+    attend_whole_back(
+        query_ref, query_t_ref, pairs_ref.at[:, :width], pairs_ref.at[:, width:], views.attn, mix_ref,
+        dmix_ref, dmix_t_ref, dquery_ref, dpairs_t_ref, views.work, views.dscores,
     )
     vectors_ref = views.vectors
     unit_first, scale_first = unit_of(views.centre_first.get()[...])
@@ -1142,6 +1180,7 @@
     step.far_out(triple=((length, 3 * width), bf16), mix=(square, bf16))
     step.heads_out(attn=(attn_shape, bf16))
     step.near_out(centre_first=(square, f32))
+    step.hold(work=((2, length, length), f32))
     triple, self_mix, self_attn, centre_first = step.run(self_forward_body, 24 * macs, 16)
 
     step = Kernel(chain, place)
@@ -1152,6 +1191,7 @@
     step.far_out(query=(square, bf16), pairs=((length, 2 * width), bf16), mix=(square, bf16))
     step.heads_out(attn=(attn_shape, bf16))
     step.near_out(centre_second=(square, f32))
+    step.hold(work=((2, length, length), f32))
     step.prefetch(ffn_in=ffn_in, ffn_out=ffn_out)
     (
         centre_first, query, pairs, cross_mix, cross_attn, centre_second, ffn_in_near, ffn_out_near,
@@ -1202,6 +1242,7 @@
     )
     step.prefetch(self_out=self_out, triple=triple, mix=self_mix)
     step.hold(
+        work=((2, length, length), f32), dscores=((2, length, length), bf16),
         first=(square, bf16), grad=(square, bf16), dquery=(square, bf16), dpairs_t=((2 * width, length), bf16), sums=((8, width), f32), turned=((128, half), f32),
     )
     memory_grad, grad_first, cross_keep, cross_send, self_out_near, triple, self_mix = step.run(cross_back_body, 48 * macs * 4, 24)

time: 120 us -> 118 us (0.983)
  Pallas kernels: 58.1 us -> 55.9 us
    pallas_call x7, Pallas kernels: 50.2 us -> 47.9 us  [run(): pl.pallas_call(kernel, out_shape=shapes, in_specs=[pl.BlockSpec(memory_sp...]
  transfers between devices with their start and end apart: 24 -> 24, of which waited for: 13 -> 13; matrix products, arithmetic and copies ran while one was open for 2% -> 2% of each run, Pallas kernels for 39% -> 38%
where the time goes in v1:
time: 118 us; the launch traced here: 117 us
  Pallas kernels  55.9 us (47%)
  waiting for transfers between devices  33.3 us (28%)
  starting transfers between devices  25 us (21%)
  local copies, waits for them, and re-layouts  2.22 us (2%)
    pallas_call x7, Pallas kernels, run(): pl.pallas_call(kernel, out_shape=shapes, in_specs=[pl.BlockSpec(memory_sp...  47.9 us
    ppermute x21, waiting for transfers between devices, send_wide(): lax.ppermute(values, 'wide', [(i, i ^ 1 << bit) for i in range(count)])  33.3 us
    ppermute x21, starting transfers between devices, send_wide(): lax.ppermute(values, 'wide', [(i, i ^ 1 << bit) for i in range(count)])  20 us
    pallas_call x21, Pallas kernels, small_kernel(): pl.pallas_call(kernel, out_shape=[jax.ShapeDtypeStruct(shape, dtype) for...  7.97 us
    ppermute x3, starting transfers between devices, other_half(): return lax.ppermute(values, 'narrow', [(0, 1), (1, 0)])  5.03 us
  transfers between devices with their start and end apart: 24, of which 13 were waited for; matrix products, arithmetic and copies ran while one was open for 2% of the time, Pallas kernels for 38%

profile of v1, /device:TPU:0, one launch (start us, length us, event | category | flops | bytes accessed | tf_op | source)
XLA Modules:
  0.0 117.3 jit_solution(4645781676126187970)
XLA Ops:
  0.6 3.0 %collective-permute-start.1 = (bf16[256,512]{1,0:T(8,128)(2,1)}, bf16[256,512]{1,0:T(8,128)(2,1)S(1)}, u32[]{:S(2)}, u32[]{:S(2)}) collective-permute-start(bf16[256,512]{1,0:T(8,128)(2,1)} %bitcast.14), channel_id=1, source_target_pairs={{0,1},{1,0},{2,3},{3,2},{4,5},{5,4},{6,7},{7,6},{8,9},{9,8},{10,11... | collective-permute-start | bytes 786440 | tf_op jit(solution)/shard_map/ppermute | solution.py:1153
  3.6 0.1 collective-permute-start
  3.7 1.9 %collective-permute-start.2 = (bf16[256,512]{1,0:T(8,128)(2,1)}, bf16[256,512]{1,0:T(8,128)(2,1)S(1)}, u32[]{:S(2)}, u32[]{:S(2)}) collective-permute-start(bf16[256,512]{1,0:T(8,128)(2,1)} %bitcast.21), channel_id=1, source_target_pairs={{0,1},{1,0},{2,3},{3,2},{4,5},{5,4},{6,7},{7,6},{8,9},{9,8},{10,11... | collective-permute-start | bytes 786440 | tf_op jit(solution)/shard_map/ppermute | solution.py:1153
  5.7 0.7 reshape.31
  6.4 0.8 concatenate.7
  7.1 0.8 concatenate.6.refs_0_
  7.9 3.5 %shard_map.263 = (bf16[512,1536]{1,0:T(8,128)(2,1)S(1)}, bf16[512,512]{1,0:T(8,128)(2,1)S(1)}, bf16[512,512]{1,0:T(8,128)(2,1)S(1)}, bf16[512,1024]{1,0:T(8,128)...) custom-call(s32[19]{0:T(128)S(1)} %concatenate.6.refs_0_, ...), custom_call_target="tpu_custom_call" | custom-call | flops 1073741824 | bytes 4718592 | tf_op jit(solution)/shard_map/pallas_call | solution.py:611
  11.4 6.4 %shard_map.264 = (bf16[512,1536]{1,0:T(8,128)(2,1)}, bf16[512,512]{1,0:T(8,128)(2,1)}, bf16[8,512,512]{2,1,0:T(8,128)(2,1)}, f32[512,512]{1,0:T(8,128)S(1)}, s32[8,128]{1,0:T(8,128)S(1)}) custom-call(s32[19]{0:T(128)S(1)} %concatenate.6.refs_0_, bf16[256,512]{1,0:T(8,128)(2,1)S(1)} %collective-permute-done.1.refs_1_.refs_7_, ...), custom_call_target="tpu_custom_call" | custom-call | flops 3221225472 | bytes 4460544 | tf_op jit(solution)/shard_map/pallas_call | solution.py:611
  17.9 0.0 collective-permute-done.refs_2_.refs_14_
  17.9 7.4 %shard_map.265 = (f32[512,512]{1,0:T(8,128)}, bf16[512,512]{1,0:T(8,128)(2,1)}, bf16[512,1024]{1,0:T(8,128)(2,1)}, bf16[512,512]{1,0:T(8,128)(2,1)}, bf16[8,512,...) custom-call(s32[19]{0:T(128)S(1)} %concatenate.6.refs_0_, ...), custom_call_target="tpu_custom_call" | custom-call | flops 3221225472 | bytes 8949760 | tf_op jit(solution)/shard_map/pallas_call | solution.py:611
  25.3 9.4 %shard_map.266 = (bf16[256,512]{1,0:T(8,128)(2,1)}, f32[512,512]{1,0:T(8,128)S(1)}, f32[8,512]{1,0:T(8,128)S(1)}, f32[1,2048]{1,0:T(1,128)S(1)}, f32[128,4096]{1...) custom-call(s32[19]{0:T(128)S(1)} %concatenate.6.refs_0_, ...), custom_call_target="tpu_custom_call" | custom-call | flops 5368709120 | bytes 6852608 | tf_op jit(solution)/shard_map/pallas_call | solution.py:611
  34.7 0.1 collective-permute-start.3
  34.8 3.1 %shard_map.267 = (f32[16,256]{1,0:T(8,128)S(1)}, f32[512,512]{1,0:T(8,128)S(1)}, bf16[512,512]{1,0:T(8,128)(2,1)S(1)}, bf16[512,512]{1,0:T(8,128)(2,1)S(1)}, bf1...) custom-call(s32[19]{0:T(128)S(1)} %concatenate.6.refs_0_, ...), custom_call_target="tpu_custom_call" | custom-call | flops 12884901888 | bytes 4780032 | tf_op jit(solution)/shard_map/pallas_call | solution.py:611
  37.9 0.4 shard_map.268
  38.3 1.7 %collective-permute-start.4 = (bf16[64,4096]{1,0:T(8,128)(2,1)S(1)}, bf16[64,4096]{1,0:T(8,128)(2,1)S(1)}, u32[]{:S(2)}, u32[]{:S(2)}) collective-permute-start(bf16[64,4096]{1,0:T(8,128)(2,1)S(1)} %get-tuple-element.172), channel_id=1, source_target_pairs={{0,4},{2,6},{4,0},{6,2},{8,12},{10,14},{12,8},{14,10},{16,20},{18,... | collective-permute-start | bytes 1572872 | tf_op jit(solution)/shard_map/ppermute | solution.py:1001
  40.0 10.4 %shard_map.269 = (f32[256,512]{1,0:T(8,128)}, f32[512,512]{1,0:T(8,128)S(1)}, f32[128,2688]{1,0:T(8,128)S(1)}, bf16[128,2688]{1,0:T(8,128)(2,1)S(1)}, bf16[512,5...) custom-call(s32[19]{0:T(128)S(1)} %concatenate.6.refs_0_, ...), custom_call_target="tpu_custom_call" | custom-call | flops 25769803776 | bytes 15781888 | tf_op jit(solution)/shard_map/pallas_call | solution.py:611
  50.4 0.3 collective-permute-start.5
  50.7 2.0 %collective-permute-done.4.refs_1_ = bf16[64,4096]{1,0:T(8,128)(2,1)S(1)} collective-permute-done((bf16[64,4096]{1,0:T(8,128)(2,1)S(1)}, bf16[64,4096]{1,0:T(8,128)(2,1)S(1)}, u32[]{:S(2)}, u32[]{:S(2)}) %collective-permute-start.4) | collective-permute-done | bytes 524320 | tf_op jit(solution)/shard_map/ppermute | solution.py:1001
  52.7 0.2 shard_map.270
  52.9 1.7 %collective-permute-start.6 = (bf16[32,4096]{1,0:T(8,128)(2,1)S(1)}, bf16[32,4096]{1,0:T(8,128)(2,1)S(1)}, u32[]{:S(2)}, u32[]{:S(2)}) collective-permute-start(bf16[32,4096]{1,0:T(8,128)(2,1)S(1)} %get-tuple-element.178), channel_id=1, source_target_pairs={{0,8},{2,10},{4,12},{6,14},{8,0},{10,2},{12,4},{14,6},{16,24},{18,... | collective-permute-start | bytes 786440 | tf_op jit(solution)/shard_map/ppermute | solution.py:1001
  54.7 0.3 shard_map.271
  55.0 1.6 %collective-permute-start.7 = (bf16[64,2688]{1,0:T(8,128)(2,1)S(1)}, bf16[64,2688]{1,0:T(8,128)(2,1)S(1)}, u32[]{:S(2)}, u32[]{:S(2)}) collective-permute-start(bf16[64,2688]{1,0:T(8,128)(2,1)S(1)} %get-tuple-element.184), channel_id=1, source_target_pairs={{0,4},{2,6},{4,0},{6,2},{8,12},{10,14},{12,8},{14,10},{16,20},{18,... | collective-permute-start | bytes 1032200 | tf_op jit(solution)/shard_map/ppermute | solution.py:1001
  56.6 4.3 %collective-permute-done.6.refs_1_ = bf16[32,4096]{1,0:T(8,128)(2,1)S(1)} collective-permute-done((bf16[32,4096]{1,0:T(8,128)(2,1)S(1)}, bf16[32,4096]{1,0:T(8,128)(2,1)S(1)}, u32[]{:S(2)}, u32[]{:S(2)}) %collective-permute-start.6) | collective-permute-done | bytes 262176 | tf_op jit(solution)/shard_map/ppermute | solution.py:1001
  60.9 0.1 shard_map.272
  61.0 2.8 %collective-permute-start.8 = (bf16[32,4096]{1,0:T(8,128)(2,1)S(1)}, bf16[32,4096]{1,0:T(8,128)(2,1)S(1)}, u32[]{:S(2)}, u32[]{:S(2)}) collective-permute-start(bf16[32,4096]{1,0:T(8,128)(2,1)S(1)} %get-tuple-element.186.refs_0_), channel_id=1, source_target_pairs={{0,16},{2,18},{4,20},{6,22},{8,24},{10,26},{12,28},{14,30},{16,0},... | collective-permute-start | bytes 786440 | tf_op jit(solution)/shard_map/ppermute | solution.py:1001
  63.7 7.7 %shard_map.273 = (f32[256,512]{1,0:T(8,128)}, f32[128,1536]{1,0:T(8,128)S(1)}, bf16[128,1536]{1,0:T(8,128)(2,1)S(1)}, s32[8,128]{1,0:T(8,128)S(1)}) custom-call(s32[19]{0:T(128)S(1)} %concatenate.6.refs_0_, f32[512,512]{1,0:T(8,128)S(1)} %get-tuple-element.165.refs_1_, bf16[512,512]{1,0:T(8,128)(2,1)S(1)} %get-tuple-element.166.refs_2_, ...), custom_call_target="tpu_custom_call" | custom-call | flops 38654705664 | bytes 9965568 | tf_op jit(solution)/shard_map/pallas_call | solution.py:611
  71.5 0.1 collective-permute-start.9
  71.5 0.2 shard_map.274
  71.7 1.6 %collective-permute-start.10 = (bf16[32,2688]{1,0:T(8,128)(2,1)S(1)}, bf16[32,2688]{1,0:T(8,128)(2,1)S(1)}, u32[]{:S(2)}, u32[]{:S(2)}) collective-permute-start(bf16[32,2688]{1,0:T(8,128)(2,1)S(1)} %get-tuple-element.192), channel_id=1, source_target_pairs={{0,8},{2,10},{4,12},{6,14},{8,0},{10,2},{12,4},{14,6},{16,24},{18,... | collective-permute-start | bytes 516104 | tf_op jit(solution)/shard_map/ppermute | solution.py:1001
  73.4 1.3 %collective-permute-done.8.refs_1_ = bf16[32,4096]{1,0:T(8,128)(2,1)S(1)} collective-permute-done((bf16[32,4096]{1,0:T(8,128)(2,1)S(1)}, bf16[32,4096]{1,0:T(8,128)(2,1)S(1)}, u32[]{:S(2)}, u32[]{:S(2)}) %collective-permute-start.8) | collective-permute-done | bytes 262176 | tf_op jit(solution)/shard_map/ppermute | solution.py:1001
  74.7 0.1 shard_map.275
  74.7 0.8 collective-permute-start.11
  75.6 0.2 shard_map.276
  75.8 1.6 %collective-permute-start.12 = (bf16[64,1536]{1,0:T(8,128)(2,1)S(1)}, bf16[64,1536]{1,0:T(8,128)(2,1)S(1)}, u32[]{:S(2)}, u32[]{:S(2)}) collective-permute-start(bf16[64,1536]{1,0:T(8,128)(2,1)S(1)} %get-tuple-element.197), channel_id=1, source_target_pairs={{0,4},{2,6},{4,0},{6,2},{8,12},{10,14},{12,8},{14,10},{16,20},{18,... | collective-permute-start | bytes 589832 | tf_op jit(solution)/shard_map/ppermute | solution.py:1001
  77.3 1.6 %collective-permute-done.10.refs_1_ = bf16[32,2688]{1,0:T(8,128)(2,1)S(1)} collective-permute-done((bf16[32,2688]{1,0:T(8,128)(2,1)S(1)}, bf16[32,2688]{1,0:T(8,128)(2,1)S(1)}, u32[]{:S(2)}, u32[]{:S(2)}) %collective-permute-start.10) | collective-permute-done | bytes 172064 | tf_op jit(solution)/shard_map/ppermute | solution.py:1001
  79.0 1.9 %collective-permute-start.13 = (bf16[32,2688]{1,0:T(8,128)(2,1)S(1)}, bf16[32,2688]{1,0:T(8,128)(2,1)S(1)}, u32[]{:S(2)}, u32[]{:S(2)}) collective-permute-start(bf16[32,2688]{1,0:T(8,128)(2,1)S(1)} %get-tuple-element.199.refs_0_), channel_id=1, source_target_pairs={{0,16},{2,18},{4,20},{6,22},{8,24},{10,26},{12,28},{14,30},{16,0},... | collective-permute-start | bytes 516104 | tf_op jit(solution)/shard_map/ppermute | solution.py:1001
  80.9 6.4 %collective-permute-done.11.refs_1_ = bf16[32,4096]{1,0:T(8,128)(2,1)S(1)} collective-permute-done((bf16[32,4096]{1,0:T(8,128)(2,1)S(1)}, bf16[32,4096]{1,0:T(8,128)(2,1)S(1)}, u32[]{:S(2)}, u32[]{:S(2)}) %collective-permute-start.11) | collective-permute-done | bytes 262176 | tf_op jit(solution)/shard_map/ppermute | solution.py:1001
  87.2 0.1 shard_map.278
  87.4 1.6 %collective-permute-start.17 = (bf16[64,4096]{1,0:T(8,128)(2,1)S(1)}, bf16[64,4096]{1,0:T(8,128)(2,1)S(1)}, u32[]{:S(2)}, u32[]{:S(2)}) collective-permute-start(bf16[64,4096]{1,0:T(8,128)(2,1)S(1)} %get-tuple-element.208.refs_0_), channel_id=1, source_target_pairs={{0,4},{2,6},{4,0},{6,2},{8,12},{10,14},{12,8},{14,10},{16,20},{18,... | collective-permute-start | bytes 1572872 | tf_op jit(solution)/shard_map/ppermute | solution.py:1001
  88.9 0.1 shard_map.279
  89.1 0.1 collective-permute-start.14
  89.2 0.1 collective-permute-done.13.refs_1_
  89.3 2.0 %collective-permute-start.15 = (bf16[32,2688]{1,0:T(8,128)(2,1)S(1)}, bf16[32,2688]{1,0:T(8,128)(2,1)S(1)}, u32[]{:S(2)}, u32[]{:S(2)}) collective-permute-start(bf16[32,2688]{1,0:T(8,128)(2,1)S(1)} %get-tuple-element.204.refs_0_), channel_id=1, source_target_pairs={{0,8},{2,10},{4,12},{6,14},{8,0},{10,2},{12,4},{14,6},{16,24},{18,... | collective-permute-start | bytes 516104 | tf_op jit(solution)/shard_map/ppermute | solution.py:1001
  91.3 3.6 %collective-permute-done.14.refs_1_ = bf16[32,1536]{1,0:T(8,128)(2,1)S(1)} collective-permute-done((bf16[32,1536]{1,0:T(8,128)(2,1)S(1)}, bf16[32,1536]{1,0:T(8,128)(2,1)S(1)}, u32[]{:S(2)}, u32[]{:S(2)}) %collective-permute-start.14) | collective-permute-done | bytes 98336 | tf_op jit(solution)/shard_map/ppermute | solution.py:1001
  94.9 0.5 collective-permute-start.16
  95.4 2.6 %collective-permute-done.15.refs_1_ = bf16[32,2688]{1,0:T(8,128)(2,1)S(1)} collective-permute-done((bf16[32,2688]{1,0:T(8,128)(2,1)S(1)}, bf16[32,2688]{1,0:T(8,128)(2,1)S(1)}, u32[]{:S(2)}, u32[]{:S(2)}) %collective-permute-start.15) | collective-permute-done | bytes 172064 | tf_op jit(solution)/shard_map/ppermute | solution.py:1001
  98.0 0.1 shard_map.282
  98.2 0.6 collective-permute-start.19
  98.8 2.3 %collective-permute-done.16.refs_1_ = bf16[32,1536]{1,0:T(8,128)(2,1)S(1)} collective-permute-done((bf16[32,1536]{1,0:T(8,128)(2,1)S(1)}, bf16[32,1536]{1,0:T(8,128)(2,1)S(1)}, u32[]{:S(2)}, u32[]{:S(2)}) %collective-permute-start.16) | collective-permute-done | bytes 98336 | tf_op jit(solution)/shard_map/ppermute | solution.py:1001
  101.1 0.1 collective-permute-start.18
  101.2 1.1 collective-permute-done.17.refs_1_
  102.3 0.2 shard_map.284
  102.4 3.3 %collective-permute-done.18.refs_1_ = bf16[32,1536]{1,0:T(8,128)(2,1)S(1)} collective-permute-done((bf16[32,1536]{1,0:T(8,128)(2,1)S(1)}, bf16[32,1536]{1,0:T(8,128)(2,1)S(1)}, u32[]{:S(2)}, u32[]{:S(2)}) %collective-permute-start.18) | collective-permute-done | bytes 98336 | tf_op jit(solution)/shard_map/ppermute | solution.py:1001
  105.8 0.1 shard_map.285
  105.9 0.5 collective-permute-start.22
  106.4 3.2 %collective-permute-done.19.refs_1_ = bf16[64,2688]{1,0:T(8,128)(2,1)S(1)} collective-permute-done((bf16[64,2688]{1,0:T(8,128)(2,1)S(1)}, bf16[64,2688]{1,0:T(8,128)(2,1)S(1)}, u32[]{:S(2)}, u32[]{:S(2)}) %collective-permute-start.19) | collective-permute-done | bytes 344096 | tf_op jit(solution)/shard_map/ppermute | solution.py:1001
  109.6 0.2 shard_map.286
  109.8 0.1 collective-permute-start.21
  109.9 2.3 %shard_map.287 = (f32[1024,512]{1,0:T(8,128)}, f32[256,2048]{1,0:T(8,128)}, s32[8,128]{1,0:T(8,128)S(1)}) custom-call(s32[8,128]{1,0:T(8,128)S(1)} %get-tuple-element.213.token_ref, bf16[128,4096]{1,0:T(8,128)(2,1)S(1)} %get-tuple-element.214.refs_0_, bf16[128,4096]{1,0:T(8,128)(2,1)S(1)} %collective-permute-done.20.refs_1_), custom_call_target="tpu_custom_call" | custom-call | flops 24999999488 | bytes 1 | tf_op jit(solution)/shard_map/pallas_call | solution.py:1016
  112.2 1.7 %shard_map.288 = (f32[256,512]{1,0:T(8,128)}, f32[256,1024]{1,0:T(8,128)}, f32[256,512]{1,0:T(8,128)}, f32[256,512]{1,0:T(8,128)}, f32[3,256]{1,0:T(4,128)}, /*i...) custom-call(s32[8,128]{1,0:T(8,128)S(1)} %get-tuple-element.215.token_ref, ...), custom_call_target="tpu_custom_call" | custom-call | flops 24999999488 | bytes 1 | tf_op jit(solution)/shard_map/pallas_call | solution.py:1016
  113.9 0.1 shard_map.289
  114.1 0.6 collective-permute-start.23
  114.6 1.3 %collective-permute-done.23.refs_1_ = bf16[128,1536]{1,0:T(8,128)(2,1)S(1)} collective-permute-done((bf16[128,1536]{1,0:T(8,128)(2,1)S(1)}, bf16[128,1536]{1,0:T(8,128)(2,1)S(1)}, u32[]{:S(2)}, u32[]{:S(2)}) %collective-permute-start.23) | collective-permute-done | bytes 393248 | tf_op jit(solution)/shard_map/ppermute | solution.py:1001
  116.0 1.3 %shard_map.290 = (f32[256,1536]{1,0:T(8,128)}, s32[8,128]{1,0:T(8,128)}) custom-call(s32[8,128]{1,0:T(8,128)S(1)} %get-tuple-element.219.token_ref, bf16[128,1536]{1,0:T(8,128)(2,1)S(1)} %get-tuple-element.220.refs_0_, bf16[128,1536]{1,0:T(8,128)(2,1)S(1)} %collective-permute-done.23.refs_1_), custom_call_target="tpu_custom_call" | custom-call | flops 24999999488 | bytes 1 | tf_op jit(solution)/shard_map/pallas_call | solution.py:1016
  (17 shorter events, 0.2 us)
Async XLA Ops:
  0.6 10.8 %collective-permute-start.1 = (bf16[256,512]{1,0:T(8,128)(2,1)}, bf16[256,512]{1,0:T(8,128)(2,1)S(1)}, u32[]{:S(2)}, u32[]{:S(2)}) collective-permute-start(bf16[256,512]{1,0:T(8,128)(2,1)} %bitcast.14), channel_id=1, source_target_pairs={{0,1},{1,0},{2,3},{3,2},{4,5},{5,4},{6,7},{7,6},{8,9},{9,8},{10,11... | collective-permute-start | bytes 786440 | tf_op jit(solution)/shard_map/ppermute | solution.py:1153
  3.6 14.2 %collective-permute-start = (bf16[256,512]{1,0:T(8,128)(2,1)}, bf16[256,512]{1,0:T(8,128)(2,1)S(1)}, u32[]{:S(2)}, u32[]{:S(2)}) collective-permute-start(bf16[256,512]{1,0:T(8,128)(2,1)} %bitcast.23), channel_id=1, source_target_pairs={{0,1},{1,0},{2,3},{3,2},{4,5},{5,4},{6,7},{7,6},{8,9},{9,8},{10,11... | collective-permute-start | bytes 786440 | tf_op jit(solution)/shard_map/ppermute | solution.py:1153
  3.7 21.6 %collective-permute-start.2 = (bf16[256,512]{1,0:T(8,128)(2,1)}, bf16[256,512]{1,0:T(8,128)(2,1)S(1)}, u32[]{:S(2)}, u32[]{:S(2)}) collective-permute-start(bf16[256,512]{1,0:T(8,128)(2,1)} %bitcast.21), channel_id=1, source_target_pairs={{0,1},{1,0},{2,3},{3,2},{4,5},{5,4},{6,7},{7,6},{8,9},{9,8},{10,11... | collective-permute-start | bytes 786440 | tf_op jit(solution)/shard_map/ppermute | solution.py:1153
  34.7 3.2 %collective-permute-start.3 = (bf16[128,4096]{1,0:T(8,128)(2,1)S(1)}, bf16[128,4096]{1,0:T(8,128)(2,1)S(1)}, u32[]{:S(2)}, u32[]{:S(2)}) collective-permute-start(bf16[128,4096]{1,0:T(8,128)(2,1)S(1)} %get-tuple-element.163), channel_id=1, source_target_pairs={{0,2},{2,0},{4,6},{6,4},{8,10},{10,8},{12,14},{14,12},{16,18},{18,... | collective-permute-start | bytes 3145736 | tf_op jit(solution)/shard_map/ppermute | solution.py:1001
  38.3 14.4 %collective-permute-start.4 = (bf16[64,4096]{1,0:T(8,128)(2,1)S(1)}, bf16[64,4096]{1,0:T(8,128)(2,1)S(1)}, u32[]{:S(2)}, u32[]{:S(2)}) collective-permute-start(bf16[64,4096]{1,0:T(8,128)(2,1)S(1)} %get-tuple-element.172), channel_id=1, source_target_pairs={{0,4},{2,6},{4,0},{6,2},{8,12},{10,14},{12,8},{14,10},{16,20},{18,... | collective-permute-start | bytes 1572872 | tf_op jit(solution)/shard_map/ppermute | solution.py:1001
  50.4 4.3 %collective-permute-start.5 = (bf16[128,2688]{1,0:T(8,128)(2,1)S(1)}, bf16[128,2688]{1,0:T(8,128)(2,1)S(1)}, u32[]{:S(2)}, u32[]{:S(2)}) collective-permute-start(bf16[128,2688]{1,0:T(8,128)(2,1)S(1)} %get-tuple-element.175), channel_id=1, source_target_pairs={{0,2},{2,0},{4,6},{6,4},{8,10},{10,8},{12,14},{14,12},{16,18},{18,... | collective-permute-start | bytes 2064392 | tf_op jit(solution)/shard_map/ppermute | solution.py:1001
  52.9 8.0 %collective-permute-start.6 = (bf16[32,4096]{1,0:T(8,128)(2,1)S(1)}, bf16[32,4096]{1,0:T(8,128)(2,1)S(1)}, u32[]{:S(2)}, u32[]{:S(2)}) collective-permute-start(bf16[32,4096]{1,0:T(8,128)(2,1)S(1)} %get-tuple-element.178), channel_id=1, source_target_pairs={{0,8},{2,10},{4,12},{6,14},{8,0},{10,2},{12,4},{14,6},{16,24},{18,... | collective-permute-start | bytes 786440 | tf_op jit(solution)/shard_map/ppermute | solution.py:1001
  55.0 16.6 %collective-permute-start.7 = (bf16[64,2688]{1,0:T(8,128)(2,1)S(1)}, bf16[64,2688]{1,0:T(8,128)(2,1)S(1)}, u32[]{:S(2)}, u32[]{:S(2)}) collective-permute-start(bf16[64,2688]{1,0:T(8,128)(2,1)S(1)} %get-tuple-element.184), channel_id=1, source_target_pairs={{0,4},{2,6},{4,0},{6,2},{8,12},{10,14},{12,8},{14,10},{16,20},{18,... | collective-permute-start | bytes 1032200 | tf_op jit(solution)/shard_map/ppermute | solution.py:1001
  61.0 13.7 %collective-permute-start.8 = (bf16[32,4096]{1,0:T(8,128)(2,1)S(1)}, bf16[32,4096]{1,0:T(8,128)(2,1)S(1)}, u32[]{:S(2)}, u32[]{:S(2)}) collective-permute-start(bf16[32,4096]{1,0:T(8,128)(2,1)S(1)} %get-tuple-element.186.refs_0_), channel_id=1, source_target_pairs={{0,16},{2,18},{4,20},{6,22},{8,24},{10,26},{12,28},{14,30},{16,0},... | collective-permute-start | bytes 786440 | tf_op jit(solution)/shard_map/ppermute | solution.py:1001
  71.5 4.1 %collective-permute-start.9 = (bf16[128,1536]{1,0:T(8,128)(2,1)S(1)}, bf16[128,1536]{1,0:T(8,128)(2,1)S(1)}, u32[]{:S(2)}, u32[]{:S(2)}) collective-permute-start(bf16[128,1536]{1,0:T(8,128)(2,1)S(1)} %get-tuple-element.189), channel_id=1, source_target_pairs={{0,2},{2,0},{4,6},{6,4},{8,10},{10,8},{12,14},{14,12},{16,18},{18,... | collective-permute-start | bytes 1179656 | tf_op jit(solution)/shard_map/ppermute | solution.py:1001
  71.7 7.2 %collective-permute-start.10 = (bf16[32,2688]{1,0:T(8,128)(2,1)S(1)}, bf16[32,2688]{1,0:T(8,128)(2,1)S(1)}, u32[]{:S(2)}, u32[]{:S(2)}) collective-permute-start(bf16[32,2688]{1,0:T(8,128)(2,1)S(1)} %get-tuple-element.192), channel_id=1, source_target_pairs={{0,8},{2,10},{4,12},{6,14},{8,0},{10,2},{12,4},{14,6},{16,24},{18,... | collective-permute-start | bytes 516104 | tf_op jit(solution)/shard_map/ppermute | solution.py:1001
  74.7 12.5 %collective-permute-start.11 = (bf16[32,4096]{1,0:T(8,128)(2,1)S(1)}, bf16[32,4096]{1,0:T(8,128)(2,1)S(1)}, u32[]{:S(2)}, u32[]{:S(2)}) collective-permute-start(bf16[32,4096]{1,0:T(8,128)(2,1)S(1)} %get-tuple-element.194.refs_0_), channel_id=1, source_target_pairs={{0,8},{2,10},{4,12},{6,14},{8,0},{10,2},{12,4},{14,6},{16,24},{18,... | collective-permute-start | bytes 786440 | tf_op jit(solution)/shard_map/ppermute | solution.py:1001
  75.8 13.2 %collective-permute-start.12 = (bf16[64,1536]{1,0:T(8,128)(2,1)S(1)}, bf16[64,1536]{1,0:T(8,128)(2,1)S(1)}, u32[]{:S(2)}, u32[]{:S(2)}) collective-permute-start(bf16[64,1536]{1,0:T(8,128)(2,1)S(1)} %get-tuple-element.197), channel_id=1, source_target_pairs={{0,4},{2,6},{4,0},{6,2},{8,12},{10,14},{12,8},{14,10},{16,20},{18,... | collective-permute-start | bytes 589832 | tf_op jit(solution)/shard_map/ppermute | solution.py:1001
  79.0 10.3 %collective-permute-start.13 = (bf16[32,2688]{1,0:T(8,128)(2,1)S(1)}, bf16[32,2688]{1,0:T(8,128)(2,1)S(1)}, u32[]{:S(2)}, u32[]{:S(2)}) collective-permute-start(bf16[32,2688]{1,0:T(8,128)(2,1)S(1)} %get-tuple-element.199.refs_0_), channel_id=1, source_target_pairs={{0,16},{2,18},{4,20},{6,22},{8,24},{10,26},{12,28},{14,30},{16,0},... | collective-permute-start | bytes 516104 | tf_op jit(solution)/shard_map/ppermute | solution.py:1001
  87.4 14.9 %collective-permute-start.17 = (bf16[64,4096]{1,0:T(8,128)(2,1)S(1)}, bf16[64,4096]{1,0:T(8,128)(2,1)S(1)}, u32[]{:S(2)}, u32[]{:S(2)}) collective-permute-start(bf16[64,4096]{1,0:T(8,128)(2,1)S(1)} %get-tuple-element.208.refs_0_), channel_id=1, source_target_pairs={{0,4},{2,6},{4,0},{6,2},{8,12},{10,14},{12,8},{14,10},{16,20},{18,... | collective-permute-start | bytes 1572872 | tf_op jit(solution)/shard_map/ppermute | solution.py:1001
  89.1 5.8 %collective-permute-start.14 = (bf16[32,1536]{1,0:T(8,128)(2,1)S(1)}, bf16[32,1536]{1,0:T(8,128)(2,1)S(1)}, u32[]{:S(2)}, u32[]{:S(2)}) collective-permute-start(bf16[32,1536]{1,0:T(8,128)(2,1)S(1)} %get-tuple-element.202), channel_id=1, source_target_pairs={{0,8},{2,10},{4,12},{6,14},{8,0},{10,2},{12,4},{14,6},{16,24},{18,... | collective-permute-start | bytes 294920 | tf_op jit(solution)/shard_map/ppermute | solution.py:1001
  89.3 8.7 %collective-permute-start.15 = (bf16[32,2688]{1,0:T(8,128)(2,1)S(1)}, bf16[32,2688]{1,0:T(8,128)(2,1)S(1)}, u32[]{:S(2)}, u32[]{:S(2)}) collective-permute-start(bf16[32,2688]{1,0:T(8,128)(2,1)S(1)} %get-tuple-element.204.refs_0_), channel_id=1, source_target_pairs={{0,8},{2,10},{4,12},{6,14},{8,0},{10,2},{12,4},{14,6},{16,24},{18,... | collective-permute-start | bytes 516104 | tf_op jit(solution)/shard_map/ppermute | solution.py:1001
  94.9 6.2 %collective-permute-start.16 = (bf16[32,1536]{1,0:T(8,128)(2,1)S(1)}, bf16[32,1536]{1,0:T(8,128)(2,1)S(1)}, u32[]{:S(2)}, u32[]{:S(2)}) collective-permute-start(bf16[32,1536]{1,0:T(8,128)(2,1)S(1)} %get-tuple-element.206.refs_0_), channel_id=1, source_target_pairs={{0,16},{2,18},{4,20},{6,22},{8,24},{10,26},{12,28},{14,30},{16,0},... | collective-permute-start | bytes 294920 | tf_op jit(solution)/shard_map/ppermute | solution.py:1001
  98.2 11.5 %collective-permute-start.19 = (bf16[64,2688]{1,0:T(8,128)(2,1)S(1)}, bf16[64,2688]{1,0:T(8,128)(2,1)S(1)}, u32[]{:S(2)}, u32[]{:S(2)}) collective-permute-start(bf16[64,2688]{1,0:T(8,128)(2,1)S(1)} %get-tuple-element.212.refs_0_), channel_id=1, source_target_pairs={{0,4},{2,6},{4,0},{6,2},{8,12},{10,14},{12,8},{14,10},{16,20},{18,... | collective-permute-start | bytes 1032200 | tf_op jit(solution)/shard_map/ppermute | solution.py:1001
  101.1 4.7 %collective-permute-start.18 = (bf16[32,1536]{1,0:T(8,128)(2,1)S(1)}, bf16[32,1536]{1,0:T(8,128)(2,1)S(1)}, u32[]{:S(2)}, u32[]{:S(2)}) collective-permute-start(bf16[32,1536]{1,0:T(8,128)(2,1)S(1)} %get-tuple-element.210.refs_0_), channel_id=1, source_target_pairs={{0,8},{2,10},{4,12},{6,14},{8,0},{10,2},{12,4},{14,6},{16,24},{18,... | collective-permute-start | bytes 294920 | tf_op jit(solution)/shard_map/ppermute | solution.py:1001
  105.9 8.0 %collective-permute-start.22 = (bf16[64,1536]{1,0:T(8,128)(2,1)S(1)}, bf16[64,1536]{1,0:T(8,128)(2,1)S(1)}, u32[]{:S(2)}, u32[]{:S(2)}) collective-permute-start(bf16[64,1536]{1,0:T(8,128)(2,1)S(1)} %get-tuple-element.218.refs_0_), channel_id=1, source_target_pairs={{0,4},{2,6},{4,0},{6,2},{8,12},{10,14},{12,8},{14,10},{16,20},{18,... | collective-permute-start | bytes 589832 | tf_op jit(solution)/shard_map/ppermute | solution.py:1001
  106.4 3.4 %collective-permute-start.20 = (bf16[128,4096]{1,0:T(8,128)(2,1)S(1)}, bf16[128,4096]{1,0:T(8,128)(2,1)S(1)}, u32[]{:S(2)}, u32[]{:S(2)}) collective-permute-start(bf16[128,4096]{1,0:T(8,128)(2,1)S(1)} %get-tuple-element.214.refs_0_), channel_id=1, source_target_pairs={{0,2},{2,0},{4,6},{6,4},{8,10},{10,8},{12,14},{14,12},{16,18},{18,... | collective-permute-start | bytes 3145736 | tf_op jit(solution)/shard_map/ppermute | solution.py:1001
  109.8 2.4 %collective-permute-start.21 = (bf16[128,2688]{1,0:T(8,128)(2,1)S(1)}, bf16[128,2688]{1,0:T(8,128)(2,1)S(1)}, u32[]{:S(2)}, u32[]{:S(2)}) collective-permute-start(bf16[128,2688]{1,0:T(8,128)(2,1)S(1)} %get-tuple-element.216.refs_0_), channel_id=1, source_target_pairs={{0,2},{2,0},{4,6},{6,4},{8,10},{10,8},{12,14},{14,12},{16,18},{18,... | collective-permute-start | bytes 2064392 | tf_op jit(solution)/shard_map/ppermute | solution.py:1001
  114.1 1.9 %collective-permute-start.23 = (bf16[128,1536]{1,0:T(8,128)(2,1)S(1)}, bf16[128,1536]{1,0:T(8,128)(2,1)S(1)}, u32[]{:S(2)}, u32[]{:S(2)}) collective-permute-start(bf16[128,1536]{1,0:T(8,128)(2,1)S(1)} %get-tuple-element.220.refs_0_), channel_id=1, source_target_pairs={{0,2},{2,0},{4,6},{6,4},{8,10},{10,8},{12,14},{14,12},{16,18},{18,... | collective-permute-start | bytes 1179656 | tf_op jit(solution)/shard_map/ppermute | solution.py:1001

commit v2 on v1

--- a/solution.py
+++ b/solution.py
@@ -839,6 +839,9 @@
     return values * half, half + half * (1.0 - half) * rise
 
 
+STRIP = 16
+
+
 def feed_body(scalars, views):
     (place_ref,) = scalars
     length, width = views.centre_second.shape
@@ -854,9 +857,14 @@
     block = width
     for begin in range(0, hidden, block):
         cols = slice(begin, begin + block)
-        inner = dot_nn(second_ref[...], in_ref[:, cols]) + vectors_ref[8 + begin // block : 9 + begin // block, :]
-        active, slope_ref[:, cols] = gelu_both(inner)
-        active_ref[:, cols] = low(active)
+        index = begin // block
+        held_ref = views.held.at[index % 2]
+        held_ref[...] = dot_nn(second_ref[...], in_ref[:, cols])
+        shift = vectors_ref[8 + index : 9 + index, :]
+        for first in range(0, length, STRIP):
+            rows = slice(first, first + STRIP)
+            active, slope_ref[rows, cols] = gelu_both(held_ref[rows, :] + shift)
+            active_ref[rows, cols] = low(active)
         total = total + dot_nn(active_ref[:, cols], out_ref[cols, :])
     unit, scale = unit_of(centred(total))
     work_ref[...] = unit * gain_of(vectors_ref, 2) + shift_of(vectors_ref, 2)
@@ -882,9 +890,15 @@
     into_second = jnp.zeros((length, width), jnp.float32)
     for begin in range(0, hidden, block):
         cols = slice(begin, begin + block)
-        grad_inner = dot_nt(outer_ref[...], out_ref[cols, :]) * slope_ref[:, cols]
-        wide_ref[:, cols] = jnp.sum(grad_inner, axis=0, keepdims=True)
-        inner_ref[:, cols] = low(grad_inner)
+        held_ref = views.held.at[begin // block % 2]
+        held_ref[...] = dot_nt(outer_ref[...], out_ref[cols, :])
+        summed = jnp.zeros((STRIP, block), jnp.float32)
+        for first in range(0, length, STRIP):
+            rows = slice(first, first + STRIP)
+            grad_inner = held_ref[rows, :] * slope_ref[rows, cols]
+            summed = summed + grad_inner
+            inner_ref[rows, cols] = low(grad_inner)
+        wide_ref[:, cols] = jnp.sum(summed, axis=0, keepdims=True)
         into_second = into_second + dot_nt(inner_ref[:, cols], in_ref[:, cols])
     grad_rows(place_ref, second_ref, (inner_ref[...],), keep, send, hidden)
     work_ref[...] = work_ref[...] + into_second
@@ -1133,7 +1147,7 @@
 
 
 ORDER = dict(a=near_first, c=near_first, d=near_first)
-SCHEDULE = ("a", "aca", "cadcadcdcdadcacdd")
+SCHEDULE = ("a", "acac", "acdadcdcdadcadcd")
 
 
 def whole_rows(
@@ -1208,7 +1222,7 @@
     step.prefetch(cross_out=cross_out, query=query)
     step.hold(
         second=(square, bf16), active=((length, hidden), bf16), slope=((length, hidden), f32), outer=(square, bf16),
-        inner=((length, hidden), bf16),
+        inner=((length, hidden), bf16), held=((2, length, width), f32),
     )
     output, grad, sums, in_sums, feed_keep, feed_send, cross_out_near, query = step.run(feed_body, 40 * macs, 26)
 

time: 118 us -> 115 us (0.975)
  waiting for transfers between devices: 33.3 us -> 25.9 us
  starting transfers between devices: 25 us -> 29.6 us
    ppermute x21, waiting for transfers between devices: 33.3 us -> 25.8 us  [send_wide(): lax.ppermute(values, 'wide', [(i, i ^ 1 << bit) for i in range(count)])]
    ppermute x21, starting transfers between devices: 20 us -> 24.6 us  [send_wide(): lax.ppermute(values, 'wide', [(i, i ^ 1 << bit) for i in range(count)])]
  transfers between devices with their start and end apart: 24 -> 24, of which waited for: 13 -> 11; matrix products, arithmetic and copies ran while one was open for 2% -> 2% of each run, Pallas kernels for 38% -> 39%
where the time goes in v2:
time: 115 us; the launch traced here: 114 us
  Pallas kernels  55.9 us (49%)
  starting transfers between devices  29.6 us (26%)
  waiting for transfers between devices  25.9 us (23%)
  local copies, waits for them, and re-layouts  2.22 us (2%)
    pallas_call x7, Pallas kernels, run(): pl.pallas_call(kernel, out_shape=shapes, in_specs=[pl.BlockSpec(memory_sp...  47.9 us
    ppermute x21, waiting for transfers between devices, send_wide(): lax.ppermute(values, 'wide', [(i, i ^ 1 << bit) for i in range(count)])  25.8 us
    ppermute x21, starting transfers between devices, send_wide(): lax.ppermute(values, 'wide', [(i, i ^ 1 << bit) for i in range(count)])  24.6 us
    pallas_call x21, Pallas kernels, small_kernel(): pl.pallas_call(kernel, out_shape=[jax.ShapeDtypeStruct(shape, dtype) for...  7.97 us
    ppermute x3, starting transfers between devices, other_half(): return lax.ppermute(values, 'narrow', [(0, 1), (1, 0)])  5.03 us
  transfers between devices with their start and end apart: 24, of which 11 were waited for; matrix products, arithmetic and copies ran while one was open for 2% of the time, Pallas kernels for 39%

profile of v2, /device:TPU:0, one launch (start us, length us, event | category | flops | bytes accessed | tf_op | source)
XLA Modules:
  0.0 114.5 jit_solution(17655919898044468809)
XLA Ops:
  0.6 3.0 %collective-permute-start.1 = (bf16[256,512]{1,0:T(8,128)(2,1)}, bf16[256,512]{1,0:T(8,128)(2,1)S(1)}, u32[]{:S(2)}, u32[]{:S(2)}) collective-permute-start(bf16[256,512]{1,0:T(8,128)(2,1)} %bitcast.14), channel_id=1, source_target_pairs={{0,1},{1,0},{2,3},{3,2},{4,5},{5,4},{6,7},{7,6},{8,9},{9,8},{10,11... | collective-permute-start | bytes 786440 | tf_op jit(solution)/shard_map/ppermute | solution.py:1167
  3.6 0.1 collective-permute-start
  3.7 1.9 %collective-permute-start.2 = (bf16[256,512]{1,0:T(8,128)(2,1)}, bf16[256,512]{1,0:T(8,128)(2,1)S(1)}, u32[]{:S(2)}, u32[]{:S(2)}) collective-permute-start(bf16[256,512]{1,0:T(8,128)(2,1)} %bitcast.21), channel_id=1, source_target_pairs={{0,1},{1,0},{2,3},{3,2},{4,5},{5,4},{6,7},{7,6},{8,9},{9,8},{10,11... | collective-permute-start | bytes 786440 | tf_op jit(solution)/shard_map/ppermute | solution.py:1167
  5.7 0.7 reshape.31
  6.4 0.8 concatenate.7
  7.1 0.8 concatenate.6.refs_0_
  7.9 3.5 %shard_map.263 = (bf16[512,1536]{1,0:T(8,128)(2,1)S(1)}, bf16[512,512]{1,0:T(8,128)(2,1)S(1)}, bf16[512,512]{1,0:T(8,128)(2,1)S(1)}, bf16[512,1024]{1,0:T(8,128)...) custom-call(s32[19]{0:T(128)S(1)} %concatenate.6.refs_0_, ...), custom_call_target="tpu_custom_call" | custom-call | flops 1073741824 | bytes 4718592 | tf_op jit(solution)/shard_map/pallas_call | solution.py:611
  11.4 0.0 collective-permute-done.1.refs_1_.refs_7_
  11.4 6.4 %shard_map.264 = (bf16[512,1536]{1,0:T(8,128)(2,1)}, bf16[512,512]{1,0:T(8,128)(2,1)}, bf16[8,512,512]{2,1,0:T(8,128)(2,1)}, f32[512,512]{1,0:T(8,128)S(1)}, s32[8,128]{1,0:T(8,128)S(1)}) custom-call(s32[19]{0:T(128)S(1)} %concatenate.6.refs_0_, bf16[256,512]{1,0:T(8,128)(2,1)S(1)} %collective-permute-done.1.refs_1_.refs_7_, ...), custom_call_target="tpu_custom_call" | custom-call | flops 3221225472 | bytes 4460544 | tf_op jit(solution)/shard_map/pallas_call | solution.py:611
  17.9 7.4 %shard_map.265 = (f32[512,512]{1,0:T(8,128)}, bf16[512,512]{1,0:T(8,128)(2,1)}, bf16[512,1024]{1,0:T(8,128)(2,1)}, bf16[512,512]{1,0:T(8,128)(2,1)}, bf16[8,512,...) custom-call(s32[19]{0:T(128)S(1)} %concatenate.6.refs_0_, ...), custom_call_target="tpu_custom_call" | custom-call | flops 3221225472 | bytes 8949760 | tf_op jit(solution)/shard_map/pallas_call | solution.py:611
  25.3 0.0 collective-permute-done.2.refs_6_
  25.3 9.4 %shard_map.266 = (bf16[256,512]{1,0:T(8,128)(2,1)}, f32[512,512]{1,0:T(8,128)S(1)}, f32[8,512]{1,0:T(8,128)S(1)}, f32[1,2048]{1,0:T(1,128)S(1)}, f32[128,4096]{1...) custom-call(s32[19]{0:T(128)S(1)} %concatenate.6.refs_0_, ...), custom_call_target="tpu_custom_call" | custom-call | flops 5368709120 | bytes 6852608 | tf_op jit(solution)/shard_map/pallas_call | solution.py:611
  34.7 0.1 collective-permute-start.3
  34.8 3.1 %shard_map.267 = (f32[16,256]{1,0:T(8,128)S(1)}, f32[512,512]{1,0:T(8,128)S(1)}, bf16[512,512]{1,0:T(8,128)(2,1)S(1)}, bf16[512,512]{1,0:T(8,128)(2,1)S(1)}, bf1...) custom-call(s32[19]{0:T(128)S(1)} %concatenate.6.refs_0_, ...), custom_call_target="tpu_custom_call" | custom-call | flops 12884901888 | bytes 4780032 | tf_op jit(solution)/shard_map/pallas_call | solution.py:611
  37.9 0.4 shard_map.268
  38.3 1.7 %collective-permute-start.4 = (bf16[64,4096]{1,0:T(8,128)(2,1)S(1)}, bf16[64,4096]{1,0:T(8,128)(2,1)S(1)}, u32[]{:S(2)}, u32[]{:S(2)}) collective-permute-start(bf16[64,4096]{1,0:T(8,128)(2,1)S(1)} %get-tuple-element.172), channel_id=1, source_target_pairs={{0,4},{2,6},{4,0},{6,2},{8,12},{10,14},{12,8},{14,10},{16,20},{18,... | collective-permute-start | bytes 1572872 | tf_op jit(solution)/shard_map/ppermute | solution.py:1015
  40.0 10.4 %shard_map.269 = (f32[256,512]{1,0:T(8,128)}, f32[512,512]{1,0:T(8,128)S(1)}, f32[128,2688]{1,0:T(8,128)S(1)}, bf16[128,2688]{1,0:T(8,128)(2,1)S(1)}, bf16[512,5...) custom-call(s32[19]{0:T(128)S(1)} %concatenate.6.refs_0_, ...), custom_call_target="tpu_custom_call" | custom-call | flops 25769803776 | bytes 15781888 | tf_op jit(solution)/shard_map/pallas_call | solution.py:611
  50.4 0.2 collective-permute-start.5
  50.6 2.0 %collective-permute-done.4.refs_1_ = bf16[64,4096]{1,0:T(8,128)(2,1)S(1)} collective-permute-done((bf16[64,4096]{1,0:T(8,128)(2,1)S(1)}, bf16[64,4096]{1,0:T(8,128)(2,1)S(1)}, u32[]{:S(2)}, u32[]{:S(2)}) %collective-permute-start.4) | collective-permute-done | bytes 524320 | tf_op jit(solution)/shard_map/ppermute | solution.py:1015
  52.7 0.2 shard_map.270
  52.9 1.7 %collective-permute-start.6 = (bf16[32,4096]{1,0:T(8,128)(2,1)S(1)}, bf16[32,4096]{1,0:T(8,128)(2,1)S(1)}, u32[]{:S(2)}, u32[]{:S(2)}) collective-permute-start(bf16[32,4096]{1,0:T(8,128)(2,1)S(1)} %get-tuple-element.178), channel_id=1, source_target_pairs={{0,8},{2,10},{4,12},{6,14},{8,0},{10,2},{12,4},{14,6},{16,24},{18,... | collective-permute-start | bytes 786440 | tf_op jit(solution)/shard_map/ppermute | solution.py:1015
  54.6 0.0 collective-permute-done.5.refs_1_
  54.7 0.3 shard_map.271
  55.0 1.6 %collective-permute-start.7 = (bf16[64,2688]{1,0:T(8,128)(2,1)S(1)}, bf16[64,2688]{1,0:T(8,128)(2,1)S(1)}, u32[]{:S(2)}, u32[]{:S(2)}) collective-permute-start(bf16[64,2688]{1,0:T(8,128)(2,1)S(1)} %get-tuple-element.181), channel_id=1, source_target_pairs={{0,4},{2,6},{4,0},{6,2},{8,12},{10,14},{12,8},{14,10},{16,20},{18,... | collective-permute-start | bytes 1032200 | tf_op jit(solution)/shard_map/ppermute | solution.py:1015
  56.6 4.3 %collective-permute-done.6.refs_1_ = bf16[32,4096]{1,0:T(8,128)(2,1)S(1)} collective-permute-done((bf16[32,4096]{1,0:T(8,128)(2,1)S(1)}, bf16[32,4096]{1,0:T(8,128)(2,1)S(1)}, u32[]{:S(2)}, u32[]{:S(2)}) %collective-permute-start.6) | collective-permute-done | bytes 262176 | tf_op jit(solution)/shard_map/ppermute | solution.py:1015
  60.9 0.1 shard_map.272
  61.0 2.8 %collective-permute-start.8 = (bf16[32,4096]{1,0:T(8,128)(2,1)S(1)}, bf16[32,4096]{1,0:T(8,128)(2,1)S(1)}, u32[]{:S(2)}, u32[]{:S(2)}) collective-permute-start(bf16[32,4096]{1,0:T(8,128)(2,1)S(1)} %get-tuple-element.186.refs_0_), channel_id=1, source_target_pairs={{0,16},{2,18},{4,20},{6,22},{8,24},{10,26},{12,28},{14,30},{16,0},... | collective-permute-start | bytes 786440 | tf_op jit(solution)/shard_map/ppermute | solution.py:1015
  63.7 0.7 collective-permute-done.7.refs_1_
  64.4 0.2 shard_map.273
  64.6 0.9 collective-permute-start.9
  65.5 7.7 %shard_map.274 = (f32[256,512]{1,0:T(8,128)}, f32[128,1536]{1,0:T(8,128)S(1)}, bf16[128,1536]{1,0:T(8,128)(2,1)S(1)}, s32[8,128]{1,0:T(8,128)S(1)}) custom-call(s32[19]{0:T(128)S(1)} %concatenate.6.refs_0_, f32[512,512]{1,0:T(8,128)S(1)} %get-tuple-element.165.refs_1_, bf16[512,512]{1,0:T(8,128)(2,1)S(1)} %get-tuple-element.166.refs_2_, ...), custom_call_target="tpu_custom_call" | custom-call | flops 38654705664 | bytes 9965568 | tf_op jit(solution)/shard_map/pallas_call | solution.py:611
  73.2 0.1 collective-permute-start.10
  73.3 1.3 %collective-permute-done.8.refs_1_ = bf16[32,4096]{1,0:T(8,128)(2,1)S(1)} collective-permute-done((bf16[32,4096]{1,0:T(8,128)(2,1)S(1)}, bf16[32,4096]{1,0:T(8,128)(2,1)S(1)}, u32[]{:S(2)}, u32[]{:S(2)}) %collective-permute-start.8) | collective-permute-done | bytes 262176 | tf_op jit(solution)/shard_map/ppermute | solution.py:1015
  74.6 0.1 shard_map.275
  74.7 0.8 collective-permute-start.11
  75.5 3.4 %collective-permute-start.13 = (bf16[32,2688]{1,0:T(8,128)(2,1)S(1)}, bf16[32,2688]{1,0:T(8,128)(2,1)S(1)}, u32[]{:S(2)}, u32[]{:S(2)}) collective-permute-start(bf16[32,2688]{1,0:T(8,128)(2,1)S(1)} %get-tuple-element.199.refs_0_), channel_id=1, source_target_pairs={{0,16},{2,18},{4,20},{6,22},{8,24},{10,26},{12,28},{14,30},{16,0},... | collective-permute-start | bytes 516104 | tf_op jit(solution)/shard_map/ppermute | solution.py:1015
  79.0 0.2 shard_map.277
  79.2 1.5 %collective-permute-start.12 = (bf16[64,1536]{1,0:T(8,128)(2,1)S(1)}, bf16[64,1536]{1,0:T(8,128)(2,1)S(1)}, u32[]{:S(2)}, u32[]{:S(2)}) collective-permute-start(bf16[64,1536]{1,0:T(8,128)(2,1)S(1)} %get-tuple-element.197), channel_id=1, source_target_pairs={{0,4},{2,6},{4,0},{6,2},{8,12},{10,14},{12,8},{14,10},{16,20},{18,... | collective-permute-start | bytes 589832 | tf_op jit(solution)/shard_map/ppermute | solution.py:1015
  80.7 5.1 %collective-permute-done.11.refs_1_ = bf16[32,4096]{1,0:T(8,128)(2,1)S(1)} collective-permute-done((bf16[32,4096]{1,0:T(8,128)(2,1)S(1)}, bf16[32,4096]{1,0:T(8,128)(2,1)S(1)}, u32[]{:S(2)}, u32[]{:S(2)}) %collective-permute-start.11) | collective-permute-done | bytes 262176 | tf_op jit(solution)/shard_map/ppermute | solution.py:1015
  85.8 0.1 shard_map.278
  86.0 1.6 %collective-permute-start.17 = (bf16[64,4096]{1,0:T(8,128)(2,1)S(1)}, bf16[64,4096]{1,0:T(8,128)(2,1)S(1)}, u32[]{:S(2)}, u32[]{:S(2)}) collective-permute-start(bf16[64,4096]{1,0:T(8,128)(2,1)S(1)} %get-tuple-element.208.refs_0_), channel_id=1, source_target_pairs={{0,4},{2,6},{4,0},{6,2},{8,12},{10,14},{12,8},{14,10},{16,20},{18,... | collective-permute-start | bytes 1572872 | tf_op jit(solution)/shard_map/ppermute | solution.py:1015
  87.6 0.1 shard_map.279
  87.8 0.1 collective-permute-start.14
  87.9 2.1 %collective-permute-start.15 = (bf16[32,2688]{1,0:T(8,128)(2,1)S(1)}, bf16[32,2688]{1,0:T(8,128)(2,1)S(1)}, u32[]{:S(2)}, u32[]{:S(2)}) collective-permute-start(bf16[32,2688]{1,0:T(8,128)(2,1)S(1)} %get-tuple-element.204.refs_0_), channel_id=1, source_target_pairs={{0,8},{2,10},{4,12},{6,14},{8,0},{10,2},{12,4},{14,6},{16,24},{18,... | collective-permute-start | bytes 516104 | tf_op jit(solution)/shard_map/ppermute | solution.py:1015
  90.0 2.5 %collective-permute-done.14.refs_1_ = bf16[32,1536]{1,0:T(8,128)(2,1)S(1)} collective-permute-done((bf16[32,1536]{1,0:T(8,128)(2,1)S(1)}, bf16[32,1536]{1,0:T(8,128)(2,1)S(1)}, u32[]{:S(2)}, u32[]{:S(2)}) %collective-permute-start.14) | collective-permute-done | bytes 98336 | tf_op jit(solution)/shard_map/ppermute | solution.py:1015
  92.5 3.9 %collective-permute-start.16 = (bf16[32,1536]{1,0:T(8,128)(2,1)S(1)}, bf16[32,1536]{1,0:T(8,128)(2,1)S(1)}, u32[]{:S(2)}, u32[]{:S(2)}) collective-permute-start(bf16[32,1536]{1,0:T(8,128)(2,1)S(1)} %get-tuple-element.206.refs_0_), channel_id=1, source_target_pairs={{0,16},{2,18},{4,20},{6,22},{8,24},{10,26},{12,28},{14,30},{16,0},... | collective-permute-start | bytes 294920 | tf_op jit(solution)/shard_map/ppermute | solution.py:1015
  96.4 0.1 shard_map.282
  96.5 0.7 collective-permute-start.19
  97.2 3.4 %collective-permute-done.16.refs_1_ = bf16[32,1536]{1,0:T(8,128)(2,1)S(1)} collective-permute-done((bf16[32,1536]{1,0:T(8,128)(2,1)S(1)}, bf16[32,1536]{1,0:T(8,128)(2,1)S(1)}, u32[]{:S(2)}, u32[]{:S(2)}) %collective-permute-start.16) | collective-permute-done | bytes 98336 | tf_op jit(solution)/shard_map/ppermute | solution.py:1015
  100.6 0.5 collective-permute-start.18
  101.2 0.2 shard_map.284
  101.3 4.0 %collective-permute-done.18.refs_1_ = bf16[32,1536]{1,0:T(8,128)(2,1)S(1)} collective-permute-done((bf16[32,1536]{1,0:T(8,128)(2,1)S(1)}, bf16[32,1536]{1,0:T(8,128)(2,1)S(1)}, u32[]{:S(2)}, u32[]{:S(2)}) %collective-permute-start.18) | collective-permute-done | bytes 98336 | tf_op jit(solution)/shard_map/ppermute | solution.py:1015
  105.3 0.1 shard_map.285
  105.4 0.7 collective-permute-start.21
  106.1 0.6 collective-permute-done.19.refs_1_
  106.7 0.2 shard_map.286
  106.9 0.1 collective-permute-start.22
  106.9 1.8 %collective-permute-done.20.refs_1_ = bf16[128,4096]{1,0:T(8,128)(2,1)S(1)} collective-permute-done((bf16[128,4096]{1,0:T(8,128)(2,1)S(1)}, bf16[128,4096]{1,0:T(8,128)(2,1)S(1)}, u32[]{:S(2)}, u32[]{:S(2)}) %collective-permute-start.20) | collective-permute-done | bytes 1048608 | tf_op jit(solution)/shard_map/ppermute | solution.py:1015
  108.7 2.3 %shard_map.287 = (f32[1024,512]{1,0:T(8,128)}, f32[256,2048]{1,0:T(8,128)}, s32[8,128]{1,0:T(8,128)S(1)}) custom-call(s32[8,128]{1,0:T(8,128)S(1)} %get-tuple-element.213.token_ref, bf16[128,4096]{1,0:T(8,128)(2,1)S(1)} %get-tuple-element.214.refs_0_, bf16[128,4096]{1,0:T(8,128)(2,1)S(1)} %collective-permute-done.20.refs_1_), custom_call_target="tpu_custom_call" | custom-call | flops 24999999488 | bytes 1 | tf_op jit(solution)/shard_map/pallas_call | solution.py:1030
  111.0 0.1 collective-permute-done.21.refs_1_
  111.2 0.1 shard_map.288
  111.3 0.1 collective-permute-start.23
  111.4 1.7 %shard_map.289 = (f32[256,512]{1,0:T(8,128)}, f32[256,1024]{1,0:T(8,128)}, f32[256,512]{1,0:T(8,128)}, f32[256,512]{1,0:T(8,128)}, f32[3,256]{1,0:T(4,128)}, /*i...) custom-call(s32[8,128]{1,0:T(8,128)S(1)} %get-tuple-element.217.token_ref, ...), custom_call_target="tpu_custom_call" | custom-call | flops 24999999488 | bytes 1 | tf_op jit(solution)/shard_map/pallas_call | solution.py:1030
  113.1 1.4 %shard_map.290 = (f32[256,1536]{1,0:T(8,128)}, s32[8,128]{1,0:T(8,128)}) custom-call(s32[8,128]{1,0:T(8,128)S(1)} %get-tuple-element.219.token_ref, bf16[128,1536]{1,0:T(8,128)(2,1)S(1)} %get-tuple-element.220.refs_0_, bf16[128,1536]{1,0:T(8,128)(2,1)S(1)} %collective-permute-done.23.refs_1_), custom_call_target="tpu_custom_call" | custom-call | flops 24999999488 | bytes 1 | tf_op jit(solution)/shard_map/pallas_call | solution.py:1030
  (17 shorter events, 0.2 us)
Async XLA Ops:
  0.6 10.8 %collective-permute-start.1 = (bf16[256,512]{1,0:T(8,128)(2,1)}, bf16[256,512]{1,0:T(8,128)(2,1)S(1)}, u32[]{:S(2)}, u32[]{:S(2)}) collective-permute-start(bf16[256,512]{1,0:T(8,128)(2,1)} %bitcast.14), channel_id=1, source_target_pairs={{0,1},{1,0},{2,3},{3,2},{4,5},{5,4},{6,7},{7,6},{8,9},{9,8},{10,11... | collective-permute-start | bytes 786440 | tf_op jit(solution)/shard_map/ppermute | solution.py:1167
  3.6 14.2 %collective-permute-start = (bf16[256,512]{1,0:T(8,128)(2,1)}, bf16[256,512]{1,0:T(8,128)(2,1)S(1)}, u32[]{:S(2)}, u32[]{:S(2)}) collective-permute-start(bf16[256,512]{1,0:T(8,128)(2,1)} %bitcast.23), channel_id=1, source_target_pairs={{0,1},{1,0},{2,3},{3,2},{4,5},{5,4},{6,7},{7,6},{8,9},{9,8},{10,11... | collective-permute-start | bytes 786440 | tf_op jit(solution)/shard_map/ppermute | solution.py:1167
  3.7 21.6 %collective-permute-start.2 = (bf16[256,512]{1,0:T(8,128)(2,1)}, bf16[256,512]{1,0:T(8,128)(2,1)S(1)}, u32[]{:S(2)}, u32[]{:S(2)}) collective-permute-start(bf16[256,512]{1,0:T(8,128)(2,1)} %bitcast.21), channel_id=1, source_target_pairs={{0,1},{1,0},{2,3},{3,2},{4,5},{5,4},{6,7},{7,6},{8,9},{9,8},{10,11... | collective-permute-start | bytes 786440 | tf_op jit(solution)/shard_map/ppermute | solution.py:1167
  34.7 3.2 %collective-permute-start.3 = (bf16[128,4096]{1,0:T(8,128)(2,1)S(1)}, bf16[128,4096]{1,0:T(8,128)(2,1)S(1)}, u32[]{:S(2)}, u32[]{:S(2)}) collective-permute-start(bf16[128,4096]{1,0:T(8,128)(2,1)S(1)} %get-tuple-element.163), channel_id=1, source_target_pairs={{0,2},{2,0},{4,6},{6,4},{8,10},{10,8},{12,14},{14,12},{16,18},{18,... | collective-permute-start | bytes 3145736 | tf_op jit(solution)/shard_map/ppermute | solution.py:1015
  38.3 14.4 %collective-permute-start.4 = (bf16[64,4096]{1,0:T(8,128)(2,1)S(1)}, bf16[64,4096]{1,0:T(8,128)(2,1)S(1)}, u32[]{:S(2)}, u32[]{:S(2)}) collective-permute-start(bf16[64,4096]{1,0:T(8,128)(2,1)S(1)} %get-tuple-element.172), channel_id=1, source_target_pairs={{0,4},{2,6},{4,0},{6,2},{8,12},{10,14},{12,8},{14,10},{16,20},{18,... | collective-permute-start | bytes 1572872 | tf_op jit(solution)/shard_map/ppermute | solution.py:1015
  50.4 4.2 %collective-permute-start.5 = (bf16[128,2688]{1,0:T(8,128)(2,1)S(1)}, bf16[128,2688]{1,0:T(8,128)(2,1)S(1)}, u32[]{:S(2)}, u32[]{:S(2)}) collective-permute-start(bf16[128,2688]{1,0:T(8,128)(2,1)S(1)} %get-tuple-element.175), channel_id=1, source_target_pairs={{0,2},{2,0},{4,6},{6,4},{8,10},{10,8},{12,14},{14,12},{16,18},{18,... | collective-permute-start | bytes 2064392 | tf_op jit(solution)/shard_map/ppermute | solution.py:1015
  52.9 8.0 %collective-permute-start.6 = (bf16[32,4096]{1,0:T(8,128)(2,1)S(1)}, bf16[32,4096]{1,0:T(8,128)(2,1)S(1)}, u32[]{:S(2)}, u32[]{:S(2)}) collective-permute-start(bf16[32,4096]{1,0:T(8,128)(2,1)S(1)} %get-tuple-element.178), channel_id=1, source_target_pairs={{0,8},{2,10},{4,12},{6,14},{8,0},{10,2},{12,4},{14,6},{16,24},{18,... | collective-permute-start | bytes 786440 | tf_op jit(solution)/shard_map/ppermute | solution.py:1015
  55.0 9.4 %collective-permute-start.7 = (bf16[64,2688]{1,0:T(8,128)(2,1)S(1)}, bf16[64,2688]{1,0:T(8,128)(2,1)S(1)}, u32[]{:S(2)}, u32[]{:S(2)}) collective-permute-start(bf16[64,2688]{1,0:T(8,128)(2,1)S(1)} %get-tuple-element.181), channel_id=1, source_target_pairs={{0,4},{2,6},{4,0},{6,2},{8,12},{10,14},{12,8},{14,10},{16,20},{18,... | collective-permute-start | bytes 1032200 | tf_op jit(solution)/shard_map/ppermute | solution.py:1015
  61.0 13.7 %collective-permute-start.8 = (bf16[32,4096]{1,0:T(8,128)(2,1)S(1)}, bf16[32,4096]{1,0:T(8,128)(2,1)S(1)}, u32[]{:S(2)}, u32[]{:S(2)}) collective-permute-start(bf16[32,4096]{1,0:T(8,128)(2,1)S(1)} %get-tuple-element.186.refs_0_), channel_id=1, source_target_pairs={{0,16},{2,18},{4,20},{6,22},{8,24},{10,26},{12,28},{14,30},{16,0},... | collective-permute-start | bytes 786440 | tf_op jit(solution)/shard_map/ppermute | solution.py:1015
  64.6 10.9 %collective-permute-start.9 = (bf16[32,2688]{1,0:T(8,128)(2,1)S(1)}, bf16[32,2688]{1,0:T(8,128)(2,1)S(1)}, u32[]{:S(2)}, u32[]{:S(2)}) collective-permute-start(bf16[32,2688]{1,0:T(8,128)(2,1)S(1)} %get-tuple-element.189), channel_id=1, source_target_pairs={{0,8},{2,10},{4,12},{6,14},{8,0},{10,2},{12,4},{14,6},{16,24},{18,... | collective-permute-start | bytes 516104 | tf_op jit(solution)/shard_map/ppermute | solution.py:1015
  73.2 5.8 %collective-permute-start.10 = (bf16[128,1536]{1,0:T(8,128)(2,1)S(1)}, bf16[128,1536]{1,0:T(8,128)(2,1)S(1)}, u32[]{:S(2)}, u32[]{:S(2)}) collective-permute-start(bf16[128,1536]{1,0:T(8,128)(2,1)S(1)} %get-tuple-element.192), channel_id=1, source_target_pairs={{0,2},{2,0},{4,6},{6,4},{8,10},{10,8},{12,14},{14,12},{16,18},{18,... | collective-permute-start | bytes 1179656 | tf_op jit(solution)/shard_map/ppermute | solution.py:1015
  74.7 11.1 %collective-permute-start.11 = (bf16[32,4096]{1,0:T(8,128)(2,1)S(1)}, bf16[32,4096]{1,0:T(8,128)(2,1)S(1)}, u32[]{:S(2)}, u32[]{:S(2)}) collective-permute-start(bf16[32,4096]{1,0:T(8,128)(2,1)S(1)} %get-tuple-element.194.refs_0_), channel_id=1, source_target_pairs={{0,8},{2,10},{4,12},{6,14},{8,0},{10,2},{12,4},{14,6},{16,24},{18,... | collective-permute-start | bytes 786440 | tf_op jit(solution)/shard_map/ppermute | solution.py:1015
  75.5 12.3 %collective-permute-start.13 = (bf16[32,2688]{1,0:T(8,128)(2,1)S(1)}, bf16[32,2688]{1,0:T(8,128)(2,1)S(1)}, u32[]{:S(2)}, u32[]{:S(2)}) collective-permute-start(bf16[32,2688]{1,0:T(8,128)(2,1)S(1)} %get-tuple-element.199.refs_0_), channel_id=1, source_target_pairs={{0,16},{2,18},{4,20},{6,22},{8,24},{10,26},{12,28},{14,30},{16,0},... | collective-permute-start | bytes 516104 | tf_op jit(solution)/shard_map/ppermute | solution.py:1015
  79.2 8.4 %collective-permute-start.12 = (bf16[64,1536]{1,0:T(8,128)(2,1)S(1)}, bf16[64,1536]{1,0:T(8,128)(2,1)S(1)}, u32[]{:S(2)}, u32[]{:S(2)}) collective-permute-start(bf16[64,1536]{1,0:T(8,128)(2,1)S(1)} %get-tuple-element.197), channel_id=1, source_target_pairs={{0,4},{2,6},{4,0},{6,2},{8,12},{10,14},{12,8},{14,10},{16,20},{18,... | collective-permute-start | bytes 589832 | tf_op jit(solution)/shard_map/ppermute | solution.py:1015
  86.0 15.2 %collective-permute-start.17 = (bf16[64,4096]{1,0:T(8,128)(2,1)S(1)}, bf16[64,4096]{1,0:T(8,128)(2,1)S(1)}, u32[]{:S(2)}, u32[]{:S(2)}) collective-permute-start(bf16[64,4096]{1,0:T(8,128)(2,1)S(1)} %get-tuple-element.208.refs_0_), channel_id=1, source_target_pairs={{0,4},{2,6},{4,0},{6,2},{8,12},{10,14},{12,8},{14,10},{16,20},{18,... | collective-permute-start | bytes 1572872 | tf_op jit(solution)/shard_map/ppermute | solution.py:1015
  87.8 4.7 %collective-permute-start.14 = (bf16[32,1536]{1,0:T(8,128)(2,1)S(1)}, bf16[32,1536]{1,0:T(8,128)(2,1)S(1)}, u32[]{:S(2)}, u32[]{:S(2)}) collective-permute-start(bf16[32,1536]{1,0:T(8,128)(2,1)S(1)} %get-tuple-element.202), channel_id=1, source_target_pairs={{0,8},{2,10},{4,12},{6,14},{8,0},{10,2},{12,4},{14,6},{16,24},{18,... | collective-permute-start | bytes 294920 | tf_op jit(solution)/shard_map/ppermute | solution.py:1015
  87.9 8.5 %collective-permute-start.15 = (bf16[32,2688]{1,0:T(8,128)(2,1)S(1)}, bf16[32,2688]{1,0:T(8,128)(2,1)S(1)}, u32[]{:S(2)}, u32[]{:S(2)}) collective-permute-start(bf16[32,2688]{1,0:T(8,128)(2,1)S(1)} %get-tuple-element.204.refs_0_), channel_id=1, source_target_pairs={{0,8},{2,10},{4,12},{6,14},{8,0},{10,2},{12,4},{14,6},{16,24},{18,... | collective-permute-start | bytes 516104 | tf_op jit(solution)/shard_map/ppermute | solution.py:1015
  92.5 8.1 %collective-permute-start.16 = (bf16[32,1536]{1,0:T(8,128)(2,1)S(1)}, bf16[32,1536]{1,0:T(8,128)(2,1)S(1)}, u32[]{:S(2)}, u32[]{:S(2)}) collective-permute-start(bf16[32,1536]{1,0:T(8,128)(2,1)S(1)} %get-tuple-element.206.refs_0_), channel_id=1, source_target_pairs={{0,16},{2,18},{4,20},{6,22},{8,24},{10,26},{12,28},{14,30},{16,0},... | collective-permute-start | bytes 294920 | tf_op jit(solution)/shard_map/ppermute | solution.py:1015
  96.5 10.1 %collective-permute-start.19 = (bf16[64,2688]{1,0:T(8,128)(2,1)S(1)}, bf16[64,2688]{1,0:T(8,128)(2,1)S(1)}, u32[]{:S(2)}, u32[]{:S(2)}) collective-permute-start(bf16[64,2688]{1,0:T(8,128)(2,1)S(1)} %get-tuple-element.212.refs_0_), channel_id=1, source_target_pairs={{0,4},{2,6},{4,0},{6,2},{8,12},{10,14},{12,8},{14,10},{16,20},{18,... | collective-permute-start | bytes 1032200 | tf_op jit(solution)/shard_map/ppermute | solution.py:1015
  100.6 4.7 %collective-permute-start.18 = (bf16[32,1536]{1,0:T(8,128)(2,1)S(1)}, bf16[32,1536]{1,0:T(8,128)(2,1)S(1)}, u32[]{:S(2)}, u32[]{:S(2)}) collective-permute-start(bf16[32,1536]{1,0:T(8,128)(2,1)S(1)} %get-tuple-element.210.refs_0_), channel_id=1, source_target_pairs={{0,8},{2,10},{4,12},{6,14},{8,0},{10,2},{12,4},{14,6},{16,24},{18,... | collective-permute-start | bytes 294920 | tf_op jit(solution)/shard_map/ppermute | solution.py:1015
  105.4 5.7 %collective-permute-start.21 = (bf16[64,1536]{1,0:T(8,128)(2,1)S(1)}, bf16[64,1536]{1,0:T(8,128)(2,1)S(1)}, u32[]{:S(2)}, u32[]{:S(2)}) collective-permute-start(bf16[64,1536]{1,0:T(8,128)(2,1)S(1)} %get-tuple-element.216.refs_0_), channel_id=1, source_target_pairs={{0,4},{2,6},{4,0},{6,2},{8,12},{10,14},{12,8},{14,10},{16,20},{18,... | collective-permute-start | bytes 589832 | tf_op jit(solution)/shard_map/ppermute | solution.py:1015
  106.1 2.7 %collective-permute-start.20 = (bf16[128,4096]{1,0:T(8,128)(2,1)S(1)}, bf16[128,4096]{1,0:T(8,128)(2,1)S(1)}, u32[]{:S(2)}, u32[]{:S(2)}) collective-permute-start(bf16[128,4096]{1,0:T(8,128)(2,1)S(1)} %get-tuple-element.214.refs_0_), channel_id=1, source_target_pairs={{0,2},{2,0},{4,6},{6,4},{8,10},{10,8},{12,14},{14,12},{16,18},{18,... | collective-permute-start | bytes 3145736 | tf_op jit(solution)/shard_map/ppermute | solution.py:1015
  106.9 4.5 %collective-permute-start.22 = (bf16[128,2688]{1,0:T(8,128)(2,1)S(1)}, bf16[128,2688]{1,0:T(8,128)(2,1)S(1)}, u32[]{:S(2)}, u32[]{:S(2)}) collective-permute-start(bf16[128,2688]{1,0:T(8,128)(2,1)S(1)} %get-tuple-element.218.refs_0_), channel_id=1, source_target_pairs={{0,2},{2,0},{4,6},{6,4},{8,10},{10,8},{12,14},{14,12},{16,18},{18,... | collective-permute-start | bytes 2064392 | tf_op jit(solution)/shard_map/ppermute | solution.py:1015
  111.3 1.8 %collective-permute-start.23 = (bf16[128,1536]{1,0:T(8,128)(2,1)S(1)}, bf16[128,1536]{1,0:T(8,128)(2,1)S(1)}, u32[]{:S(2)}, u32[]{:S(2)}) collective-permute-start(bf16[128,1536]{1,0:T(8,128)(2,1)S(1)} %get-tuple-element.220.refs_0_), channel_id=1, source_target_pairs={{0,2},{2,0},{4,6},{6,4},{8,10},{10,8},{12,14},{14,12},{16,18},{18,... | collective-permute-start | bytes 1179656 | tf_op jit(solution)/shard_map/ppermute | solution.py:1015
